TPU v7x, 256 devices: a whole 4x4x8 slice. The times are simulated.
256 devices in a mesh: row: 32 (over z, x), col: 4 (over y), rhs: 2 (over core).
Axes of the slice: x: 4, y: 4, z: 8, core: 2. Of those that a mesh axis runs over, the one named last changes fastest.
Arguments:
- vector: bfloat16 [64, 262144], P('rhs', ('row', 'col')), may hold values from -6 to 6
- near_blocks: bfloat16 [1024, 8, 256, 256], P(('row', 'col'), 'rhs'), may hold values from -0.125 to 0.125
- near_cols: int32 [1024, 8], P(('row', 'col'), 'rhs'), may hold values from 0 to 1023, as said below
- coupling: bfloat16 [32, 4, 32, 2, 128, 128], P('row', 'col'), may hold values from -0.1875 to 0.1875
- far_dst: int32 [32, 4, 32, 2], P('row', 'col'), may hold values from 0 to 31
- far_src: int32 [32, 4, 32, 2], P('row', 'col'), may hold values from 0 to 7
- row_cluster_basis: bfloat16 [1024, 256, 128], P(('row', 'col')), may hold values from -0.5 to 0.5
- column_cluster_basis: bfloat16 [1024, 256, 128], P(('row', 'col')), may hold values from -0.375 to 0.375
Outputs:
- first_image: bfloat16 [64, 262144], P('rhs', ('row', 'col'))
- second_image: bfloat16 [64, 262144], P('rhs', ('row', 'col'))
Inputs may be any that keep to these rules, and one draw needn't show every extreme that they name: near_cols[c, 0] = c, and every entry lies within 8 of its row's cluster c.
All inputs are finite; a program needn't handle non-finite values.
Results may differ from a plain program's by a relative error of at most 0.02.
Values may be sent and summed in bfloat16 or wider, within the bound.
No kernel may reach another device: no remote copies, remote signals or barrier semaphores. Data moves between devices by JAX's collectives and lax.ppermute only.
A program may use at most 64 MiB of HBM per device.

v0:
```python
import jax
import jax.numpy as jnp
from jax import lax
from jax.sharding import PartitionSpec as P


def extended(x, sides, width):
    for axis, dim in sides:
        devices, length = (lax.axis_size(axis), x.shape[dim])
        up = [(i, (i + 1) % devices) for i in range(devices - 1)]
        down = [(j, i) for i, j in up]
        last = lax.slice_in_dim(x, length - width, length, axis=dim)
        initial = lax.slice_in_dim(x, 0, width, axis=dim)
        before = lax.ppermute(last, axis, up)
        after = lax.ppermute(initial, axis, down)
        x = jnp.concatenate([before, x, after], axis=dim)
    return x


def per_device(
    vector,
    near_blocks,
    near_cols,
    coupling,
    far_dst,
    far_src,
    row_cluster_basis,
    column_cluster_basis,
):
    clusters = row_cluster_basis.shape[0]
    leaf_size = row_cluster_basis.shape[1]
    basis_rank = row_cluster_basis.shape[2]
    row_peers = lax.axis_size("row")
    slot_count = far_src.shape[3]
    couple = coupling.reshape(row_peers * slot_count, basis_rank, basis_rank)
    targets = far_dst.reshape(row_peers * slot_count)
    owned_rows = clusters * lax.axis_size("col")
    onehot = (targets[None, :] == jnp.arange(owned_rows, dtype=jnp.int32)[:, None]).astype(
        jnp.float32
    )
    src_grid = far_src.reshape(row_peers, slot_count)
    first_cluster = (lax.axis_index(("row", "col")) - 1) * clusters
    local_cols = near_cols - first_cluster
    sources = (jnp.arange(row_peers, dtype=jnp.int32)[:, None] * clusters + src_grid).reshape(
        row_peers * slot_count
    )

    def apply_once(current):
        own_cols = current.shape[0]
        whole = lax.all_gather(current, "rhs", axis=0, tiled=True)
        total_cols = whole.shape[0]
        window = extended(whole, ((("row", "col"), 1),), clusters * leaf_size)
        window = window.reshape(total_cols, 3 * clusters, leaf_size)
        taken = jnp.take(window, local_cols, axis=1)
        near_part = jnp.einsum(
            "hcsm,cslm->hcl", taken, near_blocks, preferred_element_type=jnp.float32
        )
        near_part = near_part.reshape(total_cols, clusters * leaf_size)
        near_own = lax.psum_scatter(
            near_part.astype(jnp.bfloat16), "rhs", scatter_dimension=0, tiled=True
        ).astype(jnp.float32)
        block_list = current.reshape(own_cols, clusters, leaf_size)
        coeff_own = jnp.einsum(
            "sao,aon->asn", block_list, column_cluster_basis, preferred_element_type=jnp.float32
        ).astype(jnp.bfloat16)
        gathered = lax.all_gather(coeff_own, "row", axis=0, tiled=True)
        picked = jnp.take(gathered, sources, axis=0)
        contrib = jnp.einsum("bhm,bkm->bhk", picked, couple, preferred_element_type=jnp.float32)
        partial_sums = jnp.einsum("ib,bhk->ihk", onehot, contrib, precision=lax.Precision.HIGHEST)
        coupled_terms = lax.psum_scatter(
            partial_sums.astype(jnp.bfloat16), "col", scatter_dimension=0, tiled=True
        )
        distant_contribution = jnp.einsum(
            "oba,oya->boy", coupled_terms, row_cluster_basis, preferred_element_type=jnp.float32
        )
        distant_contribution = distant_contribution.reshape(own_cols, clusters * leaf_size)
        total = 0.5 * current.astype(jnp.float32) + near_own + distant_contribution
        return total.astype(jnp.bfloat16)

    first_image = apply_once(vector)
    second_image = apply_once(first_image)
    return (first_image, second_image)


def solution(mesh):
    return jax.shard_map(
        per_device,
        mesh=mesh,
        in_specs=(
            P("rhs", ("row", "col")),
            P(("row", "col"), "rhs", None, None),
            P(("row", "col"), "rhs"),
            P("row", "col", None, None, None, None),
            P("row", "col", None, None),
            P("row", "col", None, None),
            P(("row", "col"), None, None),
            P(("row", "col"), None, None),
        ),
        out_specs=(P("rhs", ("row", "col")), P("rhs", ("row", "col"))),
        check_vma=False,
    )
```

profile of v0, /device:TPU:32, one launch (start us, length us, event | category | flops | bytes accessed | tf_op | source)
XLA Modules:
  0.0 264.9 jit_solution(18149308380864756053)
XLA Ops:
  7.2 2.1 convolution_convert_fusion.3
  9.4 2.2 all_gather.12
  11.6 6.7 %collective-permute-start.1 = (bf16[64,2048]{1,0:T(8,128)(2,1)S(1)}, bf16[64,2048]{1,0:T(8,128)(2,1)S(1)}, u32[]{:S(2)}, u32[]{:S(2)}) collective-permute-start(bf16[64,2048]{1,0:T(8,128)(2,1)S(1)} %all_gather.12), channel_id=1, source_target_pairs={{2,0},{4,2},{6,4},{8,6},{10,8},{12,10},{14,12},{16,14},{18,16},{20... | collective-permute-start | bytes 786440 | tf_op jit(solution)/shard_map/ppermute | solution.py:15
  18.2 1.9 collective-permute-start
  22.2 0.8 copy.51
  23.1 67.8 %all-gather.3.cloned.1.call-done = bf16[256,32,128]{2,1,0:T(8,128)(2,1)} async-done(((bf16[8,32,128]{2,1,0:T(8,128)(2,1)}), bf16[256,32,128]{2,1,0:T(8,128)(2,1)}) %all-gather.3.cloned.1.call-update) | async-done | bytes 2097168 | tf_op jit(solution)/shard_map/all_gather | solution.py:66
  90.9 2.2 gather_fusion.1
  93.1 1.2 fusion.16
  94.4 1.1 fusion.2
  95.5 0.8 copy.103
  96.5 1.6 gather_fusion
  98.1 3.9 %fusion.5 = bf16[8,8,8,256]{3,2,1,0:T(8,128)(2,1)S(1)} fusion(bf16[8,4,256,256]{3,2,1,0:T(8,128)(2,1)} %param.13, bf16[8,4,64,256]{3,2,1,0:T(8,128)(2,1)} %bitcast.90, pred[8,4]{1,0:T(8,128)(4,1)S(1)} %copy.46), kind=kOutput, calls=%fused_computation.13 | convolution fusion | flops 269090816 | bytes 5505056 | tf_op jit(solution)/shard_map/hcsm,cslm->hcl/dot_general | solution.py:55
  102.9 14.8 %reduce-scatter.13.cloned.1.call-done = bf16[8,4096]{1,0:T(8,128)(2,1)} async-done(((bf16[32,4096]{1,0:T(8,128)(2,1)}), bf16[8,4096]{1,0:T(8,128)(2,1)}) %reduce-scatter.13.cloned.1.call-update) | async-done | bytes 65552
  117.6 1.1 convolution_bitcast_fusion.3
  119.5 13.6 %reduce-scatter.9.cloned.1.call-done = bf16[32,2048]{1,0:T(8,128)(2,1)} async-done(((bf16[64,2048]{1,0:T(8,128)(2,1)}), bf16[32,2048]{1,0:T(8,128)(2,1)}) %reduce-scatter.9.cloned.1.call-update) | async-done | bytes 131088 | tf_op jit(solution)/shard_map/reduce_scatter | solution.py:59
  133.1 1.0 add_convert_fusion.1
  134.1 0.8 convolution_convert_fusion.2
  135.0 2.0 all_gather.14
  137.0 6.7 %collective-permute-start.3 = (bf16[64,2048]{1,0:T(8,128)(2,1)S(1)}, bf16[64,2048]{1,0:T(8,128)(2,1)}, u32[]{:S(2)}, u32[]{:S(2)}) collective-permute-start(bf16[64,2048]{1,0:T(8,128)(2,1)S(1)} %all_gather.14), channel_id=1, source_target_pairs={{2,0},{4,2},{6,4},{8,6},{10,8},{12,10},{14,12},{16,14},{18,16},{20... | collective-permute-start | bytes 786440 | tf_op jit(solution)/shard_map/ppermute | solution.py:15
  143.7 1.9 collective-permute-start.2
  145.6 68.8 %all-gather.5.cloned.1.call-done = bf16[256,32,128]{2,1,0:T(8,128)(2,1)} async-done(((bf16[8,32,128]{2,1,0:T(8,128)(2,1)}), bf16[256,32,128]{2,1,0:T(8,128)(2,1)}) %all-gather.5.cloned.1.call-update) | async-done | bytes 2097168 | tf_op jit(solution)/shard_map/all_gather | solution.py:66
  214.5 2.2 gather_fusion.3
  216.7 1.2 fusion.14
  218.0 1.1 fusion.3
  219.1 0.8 copy.102
  219.9 1.1 pad_maximum_fusion.1
  221.1 1.6 gather_fusion.2
  222.7 3.9 %fusion.4 = bf16[8,8,8,256]{3,2,1,0:T(8,128)(2,1)S(1)} fusion(bf16[8,4,256,256]{3,2,1,0:T(8,128)(2,1)} %param.13, bf16[8,4,64,256]{3,2,1,0:T(8,128)(2,1)} %bitcast.89, pred[8,4]{1,0:T(8,128)(4,1)S(1)} %copy-done.6), kind=kOutput, calls=%fused_computation.12 | convolution fusion | flops 269090816 | bytes 5505056 | tf_op jit(solution)/shard_map/hcsm,cslm->hcl/dot_general | solution.py:55
  227.4 13.9 %reduce-scatter.15.cloned.1.call-done = bf16[8,4096]{1,0:T(8,128)(2,1)} async-done(((bf16[32,4096]{1,0:T(8,128)(2,1)}), bf16[8,4096]{1,0:T(8,128)(2,1)}) %reduce-scatter.15.cloned.1.call-update) | async-done | bytes 65552
  241.2 1.1 convolution_bitcast_fusion.2
  242.3 14.1 %reduce-scatter.11.cloned.1.call-done = bf16[32,2048]{1,0:T(8,128)(2,1)} async-done(((bf16[64,2048]{1,0:T(8,128)(2,1)}), bf16[32,2048]{1,0:T(8,128)(2,1)}) %reduce-scatter.11.cloned.1.call-update) | async-done | bytes 131088 | tf_op jit(solution)/shard_map/reduce_scatter | solution.py:59
  256.4 1.6 add_convert_fusion
  (50 shorter events, 4.9 us)
Async XLA Ops:
  7.2 86.0 %copy-start = (bf16[1,1,32,2,128,128]{5,4,3,2,1,0:T(8,128)(2,1)S(1)}, bf16[1,1,32,2,128,128]{5,4,3,2,1,0:T(8,128)(2,1)}, u32[]{:S(2)}) copy-start(bf16[1,1,32,2,128,128]{5,4,3,2,1,0:T(8,128)(2,1)} %param.15) | copy-start | bytes 6291460
  7.2 83.7 %all-gather.3.cloned.1.call-start = ((), (), s32[]{:S(2)}) async-start(), calls=%async_computation.5 | async-start | bytes 2162688 | tf_op jit(solution)/shard_map/all_gather | solution.py:66
  9.3 108.3 %reduce-scatter.13.cloned.1.call-start = ((), (), s32[]{:S(2)}) async-start(), calls=%async_computation.8 | async-start | bytes 327680
  11.6 84.8 %collective-permute-start.1 = (bf16[64,2048]{1,0:T(8,128)(2,1)S(1)}, bf16[64,2048]{1,0:T(8,128)(2,1)S(1)}, u32[]{:S(2)}, u32[]{:S(2)}) collective-permute-start(bf16[64,2048]{1,0:T(8,128)(2,1)S(1)} %all_gather.12), channel_id=1, source_target_pairs={{2,0},{4,2},{6,4},{8,6},{10,8},{12,10},{14,12},{16,14},{18,16},{20... | collective-permute-start | bytes 786440 | tf_op jit(solution)/shard_map/ppermute | solution.py:15
  18.2 78.1 %collective-permute-start = (bf16[64,2048]{1,0:T(8,128)(2,1)S(1)}, bf16[64,2048]{1,0:T(8,128)(2,1)S(1)}, u32[]{:S(2)}, u32[]{:S(2)}) collective-permute-start(bf16[64,2048]{1,0:T(8,128)(2,1)S(1)} %all_gather.12), channel_id=1, source_target_pairs={{0,2},{2,4},{4,6},{6,8},{8,10},{10,12},{12,14},{14,16},{16,18},{18... | collective-permute-start | bytes 786440 | tf_op jit(solution)/shard_map/ppermute | solution.py:14
  21.0 77.1 %copy-start.5 = (pred[8,4]{1,0:T(8,128)(4,1)}, pred[8,4]{1,0:T(8,128)(4,1)S(1)}, u32[]{:S(2)}) copy-start(pred[8,4]{1,0:T(8,128)(4,1)S(1)} %copy.46) | copy-start | bytes 100
  96.3 36.8 %reduce-scatter.9.cloned.1.call-start = ((), (), s32[]{:S(2)}) async-start(), calls=%async_computation.4 | async-start | bytes 393216 | tf_op jit(solution)/shard_map/reduce_scatter | solution.py:59
  98.1 19.5 %copy-start.3 = (bf16[8,256,128]{2,1,0:T(8,128)(2,1)S(1)}, bf16[8,256,128]{2,1,0:T(8,128)(2,1)}, u32[]{:S(2)}) copy-start(bf16[8,256,128]{2,1,0:T(8,128)(2,1)} %param.18) | copy-start | bytes 1572868
  102.1 31.0 %copy-start.4 = (bf16[32,2048]{1,0:T(8,128)(2,1)S(1)}, bf16[32,2048]{1,0:T(8,128)(2,1)}, u32[]{:S(2)}) copy-start(bf16[32,2048]{1,0:T(8,128)(2,1)} %param.12) | copy-start | bytes 393220
  102.1 32.0 %copy-start.2 = (bf16[8,256,128]{2,1,0:T(8,128)(2,1)S(1)}, bf16[8,256,128]{2,1,0:T(8,128)(2,1)}, u32[]{:S(2)}) copy-start(bf16[8,256,128]{2,1,0:T(8,128)(2,1)} %param.19) | copy-start | bytes 1572868
  102.8 111.7 %all-gather.5.cloned.1.call-start = ((), (), s32[]{:S(2)}) async-start(), calls=%async_computation.7 | async-start | bytes 2162688 | tf_op jit(solution)/shard_map/all_gather | solution.py:66
  134.1 122.3 %copy-start.1 = (bf16[32,2048]{1,0:T(8,128)(2,1)}, bf16[32,2048]{1,0:T(8,128)(2,1)S(1)}, u32[]{:S(2)}) copy-start(bf16[32,2048]{1,0:T(8,128)(2,1)S(1)} %add_convert_fusion.1) | copy-start | bytes 393220
  135.0 106.2 %reduce-scatter.15.cloned.1.call-start = ((), (), s32[]{:S(2)}) async-start(), calls=%async_computation.9 | async-start | bytes 327680
  137.0 82.9 %collective-permute-start.3 = (bf16[64,2048]{1,0:T(8,128)(2,1)S(1)}, bf16[64,2048]{1,0:T(8,128)(2,1)}, u32[]{:S(2)}, u32[]{:S(2)}) collective-permute-start(bf16[64,2048]{1,0:T(8,128)(2,1)S(1)} %all_gather.14), channel_id=1, source_target_pairs={{2,0},{4,2},{6,4},{8,6},{10,8},{12,10},{14,12},{16,14},{18,16},{20... | collective-permute-start | bytes 786440 | tf_op jit(solution)/shard_map/ppermute | solution.py:15
  143.7 76.2 %collective-permute-start.2 = (bf16[64,2048]{1,0:T(8,128)(2,1)S(1)}, bf16[64,2048]{1,0:T(8,128)(2,1)}, u32[]{:S(2)}, u32[]{:S(2)}) collective-permute-start(bf16[64,2048]{1,0:T(8,128)(2,1)S(1)} %all_gather.14), channel_id=1, source_target_pairs={{0,2},{2,4},{4,6},{6,8},{8,10},{10,12},{12,14},{14,16},{16,18},{18... | collective-permute-start | bytes 786440 | tf_op jit(solution)/shard_map/ppermute | solution.py:14
  219.9 36.6 %reduce-scatter.11.cloned.1.call-start = ((), (), s32[]{:S(2)}) async-start(), calls=%async_computation.6 | async-start | bytes 393216 | tf_op jit(solution)/shard_map/reduce_scatter | solution.py:59
  221.0 1.7 copy-start.6
Sparse Core Ops, SparseCore 0:
  11.2 79.6 all-gather.2
  96.4 21.1 reduce-scatter.12
  120.3 12.7 reduce-scatter.8
  136.1 78.3 all-gather.4
  220.0 21.1 reduce-scatter.14
  243.7 12.6 reduce-scatter.10
where the time goes:
time: 267 us; the launch traced here: 265 us
  waiting for transfers between devices  193 us (72%)
  matrix products  17.7 us (7%)
  starting transfers between devices  17.4 us (7%)
  between operations  14.4 us (5%)
  local copies, waits for them, and re-layouts  13.8 us (5%)
  other arithmetic  4.5 us (2%)
  blocking collectives  4.2 us (2%)
    all_gather x2, waiting for transfers between devices, apply_once(): gathered = lax.all_gather(coeff_own, 'row', axis=0, tiled=True)  137 us
    unnamed x8, waiting for transfers between devices  28.7 us
    reduce_scatter x2, waiting for transfers between devices, apply_once(): lax.psum_scatter(near_part.astype(jnp.bfloat16), 'rhs', scatter_dimension...  27.7 us
    ppermute x2, starting transfers between devices, extended(): after = lax.ppermute(initial, axis, down)  13.3 us
    dot_general x2, matrix products, apply_once(): jnp.einsum('hcsm,cslm->hcl', taken, near_blocks, preferred_element_type=j...  7.84 us
  transfers between devices with their start and end apart: 10, of which 6 were waited for; matrix products, arithmetic and copies ran while one was open for 11% of the time, Pallas kernels for 0%

commit v1 on v0

v1 whole, which is shorter than its diff:
```python
import jax
import jax.numpy as jnp
from jax import lax
from jax.sharding import PartitionSpec as P


def per_device(
    vector,
    near_blocks,
    near_cols,
    coupling,
    far_dst,
    far_src,
    row_cluster_basis,
    column_cluster_basis,
):
    clusters, leaf_size, basis_rank = row_cluster_basis.shape
    row_peers = lax.axis_size("row")
    col_peers = lax.axis_size("col")
    slot_count = far_src.shape[3]
    pairs = row_peers * slot_count
    own_cols = vector.shape[0]
    couple = coupling.reshape(pairs, basis_rank, basis_rank)
    targets = far_dst.reshape(pairs)
    owned_rows = clusters * col_peers
    onehot = (targets[None, :] == jnp.arange(owned_rows, dtype=jnp.int32)[:, None]).astype(
        jnp.float32
    )
    wanted = lax.all_to_all(far_src.reshape(row_peers, slot_count), "row", 0, 0)
    wanted = wanted.reshape(pairs)

    other = [(0, 1), (1, 0)]
    first_cluster = (lax.axis_index(("row", "col")) - 1) * clusters
    local_cols = near_cols - first_cluster
    far_cols = lax.ppermute(local_cols, "rhs", other)
    far_blocks = lax.ppermute(near_blocks, "rhs", other)
    col = lax.axis_index("col")
    line = row_peers * col_peers
    up = [(i, i + 1) for i in range(line - 1)]
    down = [(j, i) for i, j in up]

    def apply_once(current):
        before = lax.ppermute(current[:, -clusters * leaf_size :], ("row", "col"), up)
        after = lax.ppermute(current[:, : clusters * leaf_size], ("row", "col"), down)
        window = jnp.concatenate([before, current, after], axis=1)
        window = window.reshape(own_cols, 3 * clusters, leaf_size)

        def near_of(cols, blocks):
            taken = jnp.take(window, cols, axis=1, mode="clip")
            return jnp.einsum("hcsm,cslm->hcl", taken, blocks, preferred_element_type=jnp.float32)

        near = near_of(local_cols, near_blocks) + near_of(far_cols, far_blocks)

        leaves = current.reshape(own_cols, clusters, leaf_size)
        coeffs = jnp.einsum(
            "sao,aon->asn", leaves, column_cluster_basis, preferred_element_type=jnp.float32
        ).astype(jnp.bfloat16)
        packed = jnp.take(coeffs, wanted, axis=0, mode="clip")
        packed = packed.reshape(row_peers, slot_count * own_cols, basis_rank)
        picked = lax.all_to_all(packed, "row", 0, 0).reshape(pairs, own_cols, basis_rank)
        contrib = jnp.einsum("bhm,bkm->bhk", picked, couple, preferred_element_type=jnp.float32)
        sums = jnp.einsum("ib,bhk->ihk", onehot, contrib, precision=lax.Precision.HIGHEST)
        sums = sums.astype(jnp.bfloat16).reshape(
            col_peers, clusters * own_cols, basis_rank
        )
        total = lax.dynamic_index_in_dim(sums, col, 0, keepdims=False).astype(jnp.float32)
        for step in range(1, col_peers):
            part = lax.dynamic_index_in_dim(
                sums, lax.rem(col + step, col_peers), 0, keepdims=False
            )
            ring = [(i, (i + step) % col_peers) for i in range(col_peers)]
            total = total + lax.ppermute(part, "col", ring).astype(jnp.float32)
        coupled = total.astype(jnp.bfloat16).reshape(clusters, own_cols, basis_rank)
        distant = jnp.einsum(
            "oba,oya->boy", coupled, row_cluster_basis, preferred_element_type=jnp.float32
        )
        image = 0.5 * leaves.astype(jnp.float32) + near + distant
        return image.astype(jnp.bfloat16).reshape(own_cols, clusters * leaf_size)

    first_image = apply_once(vector)
    second_image = apply_once(first_image)
    return (first_image, second_image)


def solution(mesh):
    return jax.shard_map(
        per_device,
        mesh=mesh,
        in_specs=(
            P("rhs", ("row", "col")),
            P(("row", "col"), "rhs", None, None),
            P(("row", "col"), "rhs"),
            P("row", "col", None, None, None, None),
            P("row", "col", None, None),
            P("row", "col", None, None),
            P(("row", "col"), None, None),
            P(("row", "col"), None, None),
        ),
        out_specs=(P("rhs", ("row", "col")), P("rhs", ("row", "col"))),
        check_vma=False,
    )
```

time: 267 us -> 112 us (0.42)
  waiting for transfers between devices: 193 us -> 30.5 us
  starting transfers between devices: 17.4 us -> 44.1 us
  between operations: 14.4 us -> 1.03 us
  blocking collectives: 4.2 us -> 0 us
    all_gather x2 -> x0, waiting for transfers between devices: 137 us -> none  [apply_once(): gathered = lax.all_gather(coeff_own, 'row', axis=0, tiled=True)]
    unnamed x8 -> x0, waiting for transfers between devices: 28.7 us -> none
    reduce_scatter x2 -> x0, waiting for transfers between devices: 27.7 us -> none  [apply_once(): lax.psum_scatter(near_part.astype(jnp.bfloat16), 'rhs', scatter_dimension...]
    all_to_all x0 -> x3, starting transfers between devices: none -> 20 us  [the longest x2 10.1 us: apply_once(): lax.all_to_all(packed, 'row', 0, 0).reshape(pairs, own_cols, basis_rank)]
    all_to_all x0 -> x3, waiting for transfers between devices: none -> 19.7 us  [the longest x2 12.6 us: apply_once(): lax.all_to_all(packed, 'row', 0, 0).reshape(pairs, own_cols, basis_rank)]
    ppermute x4 -> x12, waiting for transfers between devices: 0.01 us -> 10.8 us  [the longest x2 6.35 us: apply_once(): lax.ppermute(current[:, -clusters * leaf_size:], ('row', 'col'), up)]
    ppermute x4 -> x12, starting transfers between devices: 17.2 us -> 24 us  [the longest x2 13 us: apply_once(): lax.ppermute(current[:, :clusters * leaf_size], ('row', 'col'), down)]
    all_gather x2 -> x0, blocking collectives: 4.2 us -> none  [apply_once(): whole = lax.all_gather(current, 'rhs', axis=0, tiled=True)]
  transfers between devices with their start and end apart: 10 -> 15, of which waited for: 6 -> 8; matrix products, arithmetic and copies ran while one was open for 11% -> 24% of each run, Pallas kernels for 0% -> 0%
where the time goes in v1:
time: 112 us
  starting transfers between devices  44.1 us (39%)
  waiting for transfers between devices  30.5 us (27%)
  matrix products  19.6 us (18%)
  local copies, waits for them, and re-layouts  13.2 us (12%)
  other arithmetic  3.39 us (3%)
    ppermute x2, starting transfers between devices, apply_once(): lax.ppermute(current[:, :clusters * leaf_size], ('row', 'col'), down)  13 us
    dot_general x4, matrix products, near_of(): jnp.einsum('hcsm,cslm->hcl', taken, blocks, preferred_element_type=jnp.fl...  12.9 us
    all_to_all x2, waiting for transfers between devices, apply_once(): lax.all_to_all(packed, 'row', 0, 0).reshape(pairs, own_cols, basis_rank)  12.6 us
    all_to_all x2, starting transfers between devices, apply_once(): lax.all_to_all(packed, 'row', 0, 0).reshape(pairs, own_cols, basis_rank)  10.1 us
    all_to_all x1, starting transfers between devices, per_device(): wanted = lax.all_to_all(far_src.reshape(row_peers, slot_count), 'row', 0, 0)  9.94 us
    all_to_all x1, waiting for transfers between devices, per_device(): wanted = lax.all_to_all(far_src.reshape(row_peers, slot_count), 'row', 0, 0)  7.14 us
    ppermute x2, waiting for transfers between devices, apply_once(): lax.ppermute(current[:, -clusters * leaf_size:], ('row', 'col'), up)  6.35 us
    ppermute x2, starting transfers between devices, apply_once(): lax.ppermute(current[:, -clusters * leaf_size:], ('row', 'col'), up)  5.54 us
  transfers between devices with their start and end apart: 15, of which 8 were waited for; matrix products, arithmetic and copies ran while one was open for 24% of the time, Pallas kernels for 0%

profile of v1, /device:TPU:32, one launch (start us, length us, event | category | flops | bytes accessed | tf_op | source)
XLA Modules:
  0.0 111.7 jit_solution(3170936792293891358)
XLA Ops:
  0.7 3.6 %collective-permute-start = (bf16[32,2048]{1,0:T(8,128)(2,1)}, bf16[32,2048]{1,0:T(8,128)(2,1)S(1)}, u32[]{:S(2)}, u32[]{:S(2)}) collective-permute-start(bf16[32,2048]{1,0:T(8,128)(2,1)} %param.8), channel_id=1, source_target_pairs={{0,2},{2,4},{4,6},{6,8},{8,10},{10,12},{12,14},{14,16},{16,18},{18... | collective-permute-start | bytes 393224 | tf_op jit(solution)/shard_map/ppermute | solution.py:43
  4.4 6.6 %collective-permute-start.1 = (bf16[32,2048]{1,0:T(8,128)(2,1)}, bf16[32,2048]{1,0:T(8,128)(2,1)S(1)}, u32[]{:S(2)}, u32[]{:S(2)}) collective-permute-start(bf16[32,2048]{1,0:T(8,128)(2,1)} %param.8), channel_id=1, source_target_pairs={{2,0},{4,2},{6,4},{8,6},{10,8},{12,10},{14,12},{16,14},{18,16},{20... | collective-permute-start | bytes 393224 | tf_op jit(solution)/shard_map/ppermute | solution.py:44
  11.0 1.4 %copy.51 = s32[32,1,2]{2,1,0:T(1,128)} copy(s32[32,1,2]{0,2,1:T(2,128)} %bitcast.161) | data formatting | bytes 512 | tf_op jit(solution)/shard_map/all_to_all | solution.py:29
  12.3 9.9 %all-to-all-start = ((s32[32,1,2]{2,1,0:T(1,128)}), s32[32,1,2]{2,1,0:T(1,128)S(1)}, u32[]{:S(2)}, u32[]{:S(2)}) async-start(s32[32,1,2]{2,1,0:T(1,128)} %copy.51), calls=%async_computation | async-start | bytes 32768 | tf_op jit(solution)/shard_map/all_to_all | solution.py:29
  22.3 1.3 %convolution_convert_fusion.3 = bf16[8,32,128]{2,1,0:T(8,128)(2,1)S(1)} fusion(bf16[8,256,128]{2,1,0:T(8,128)(2,1)} %param.15, bf16[4,8,8,256]{3,2,1,0:T(8,128)(2,1)} %bitcast.145), kind=kOutput, calls=%fused_computation.26 | convolution fusion | flops 16809984 | bytes 720896 | tf_op jit(solution)/shard_map/sao,aon->asn/dot_general | solution.py:55
  23.6 7.1 %all-to-all-done = s32[32,1,2]{2,1,0:T(1,128)S(1)} async-done(((s32[32,1,2]{2,1,0:T(1,128)}), s32[32,1,2]{2,1,0:T(1,128)S(1)}, u32[]{:S(2)}, u32[]{:S(2)}) %all-to-all-start) | async-done | bytes 288 | tf_op jit(solution)/shard_map/all_to_all | solution.py:29
  32.1 1.4 %gather_fusion.2 = bf16[64,32,128]{2,1,0:T(8,128)(2,1)} fusion(bf16[8,32,128]{2,1,0:T(8,128)(2,1)S(1)} %convolution_convert_fusion.3, s32[1024]{0:T(1024)S(1)} %pad_clamp_fusion), kind=kCustom, calls=%fused_computation.2 | custom fusion | bytes 1048832 | tf_op jit(solution)/shard_map/jit(_take)/gather | solution.py:58
  33.5 5.0 %all-to-all-start.1 = ((bf16[32,64,128]{2,1,0:T(8,128)(2,1)}), bf16[32,64,128]{2,1,0:T(8,128)(2,1)S(1)}, u32[]{:S(2)}, u32[]{:S(2)}) async-start(bf16[32,64,128]{2,1,0:T(8,128)(2,1)} %bitcast.11), calls=%async_computation.1 | async-start | bytes 1048576 | tf_op jit(solution)/shard_map/all_to_all | solution.py:60
  39.4 0.8 copy.49
  40.5 0.9 pad_maximum_fusion
  42.1 12.6 %all-to-all-done.1 = bf16[32,64,128]{2,1,0:T(8,128)(2,1)S(1)} async-done(((bf16[32,64,128]{2,1,0:T(8,128)(2,1)}), bf16[32,64,128]{2,1,0:T(8,128)(2,1)S(1)}, u32[]{:S(2)}, u32[]{:S(2)}) %all-to-all-start.1) | async-done | bytes 524320 | tf_op jit(solution)/shard_map/all_to_all | solution.py:60
  54.7 1.2 %fusion.26 = f32[64,32,128]{2,1,0:T(8,128)S(1)} fusion(bf16[64,32,128]{2,1,0:T(8,128)(2,1)S(1)} %bitcast.138, bf16[64,128,128]{2,1,0:T(8,128)(2,1)S(1)} %bitcast.133), kind=kOutput, calls=%fused_computation.58 | convolution fusion | flops 67108864 | bytes 3670016 | tf_op jit(solution)/shard_map/bhm,bkm->bhk/dot_general | solution.py:61
  55.9 1.1 convolution_convert_fusion.1
  58.5 1.5 %collective-permute-start.5 = (bf16[256,128]{1,0:T(8,128)(2,1)}, bf16[256,128]{1,0:T(8,128)(2,1)}, u32[]{:S(2)}, u32[]{:S(2)}) collective-permute-start(bf16[256,128]{1,0:T(8,128)(2,1)} %get-tuple-element.7), channel_id=1, source_target_pairs={{0,4},{2,6},{4,0},{6,2},{1,5},{3,7},{5,1},{7,3},{8,12},{10,14},{12... | collective-permute-start | bytes 196616 | tf_op jit(solution)/shard_map/ppermute | solution.py:72
  60.0 1.7 %collective-permute-start.6 = (bf16[256,128]{1,0:T(8,128)(2,1)}, bf16[256,128]{1,0:T(8,128)(2,1)}, u32[]{:S(2)}, u32[]{:S(2)}) collective-permute-start(bf16[256,128]{1,0:T(8,128)(2,1)} %get-tuple-element.6), channel_id=1, source_target_pairs={{0,6},{2,0},{4,2},{6,4},{1,7},{3,1},{5,3},{7,5},{8,14},{10,8},{12,... | collective-permute-start | bytes 196616 | tf_op jit(solution)/shard_map/ppermute | solution.py:72
  61.7 2.0 %convolution_bitcast_fusion.5 = f32[8,32,256]{2,1,0:T(8,128)} fusion(bf16[32,8,4,256]{3,0,2,1:T(8,128)(2,1)S(1)} %bitcast.140, bf16[8,4,256,256]{3,2,1,0:T(8,128)(2,1)S(1)} %copy-done.1), kind=kOutput, calls=%fused_computation.21 | convolution fusion | flops 134217728 | bytes 4980736 | tf_op jit(solution)/shard_map/hcsm,cslm->hcl/dot_general | solution.py:50
  63.8 1.4 %gather_fusion.1 = bf16[32,32,256]{2,1,0:T(8,128)(2,1)} fusion(bf16[32,24,256]{2,0,1:T(8,128)(2,1)S(1)} %bitcast.136, s32[1024]{0:T(1024)S(1)} %pad_clamp_fusion.1), kind=kCustom, calls=%fused_computation.1 | custom fusion | bytes 1048704 | tf_op jit(solution)/shard_map/jit(_take)/gather | solution.py:49
  65.8 1.0 fusion.19
  66.8 3.7 %fusion.7 = f32[32,8,256]{2,0,1:T(8,128)S(1)} fusion(f32[8,32,256]{2,1,0:T(8,128)} %convolution_bitcast_fusion.5, bf16[32,8,4,256]{3,0,2,1:T(8,128)(2,1)} %bitcast.143, bf16[8,4,256,256]{3,2,1,0:T(8,128)(2,1)} %collective-permute-done.3, bf16[4,8,8,256]{3,2,1,0:T(8,128)(2,1)S(1)} %bitcast.146), kind=kOutput, calls=%fused_computation.20 | convolution fusion | flops 134479872 | bytes 5373952 | tf_op jit(solution)/shard_map/hcsm,cslm->hcl/dot_general | solution.py:50
  71.0 1.4 %gather_fusion.5 = bf16[64,32,128]{2,1,0:T(8,128)(2,1)} fusion(bf16[8,32,128]{2,1,0:T(8,128)(2,1)S(1)} %convolution_convert_fusion.2, s32[1024]{0:T(1024)S(1)} %pad_clamp_fusion), kind=kCustom, calls=%fused_computation.5 | custom fusion | bytes 1048832 | tf_op jit(solution)/shard_map/jit(_take)/gather | solution.py:58
  72.5 5.1 %all-to-all-start.2 = ((bf16[32,64,128]{2,1,0:T(8,128)(2,1)}), bf16[32,64,128]{2,1,0:T(8,128)(2,1)S(1)}, u32[]{:S(2)}, u32[]{:S(2)}) async-start(bf16[32,64,128]{2,1,0:T(8,128)(2,1)} %bitcast.30), calls=%async_computation.2 | async-start | bytes 1048576 | tf_op jit(solution)/shard_map/all_to_all | solution.py:60
  77.6 6.4 %collective-permute-start.8 = (bf16[32,2048]{1,0:T(8,128)(2,1)S(1)}, bf16[32,2048]{1,0:T(8,128)(2,1)S(1)}, u32[]{:S(2)}, u32[]{:S(2)}) collective-permute-start(bf16[32,2048]{1,0:T(8,128)(2,1)S(1)} %bitcast.155), channel_id=1, source_target_pairs={{2,0},{4,2},{6,4},{8,6},{10,8},{12,10},{14,12},{16,14},{18,16},{20... | collective-permute-start | bytes 393224 | tf_op jit(solution)/shard_map/ppermute | solution.py:44
  84.0 1.9 %collective-permute-start.7 = (bf16[32,2048]{1,0:T(8,128)(2,1)S(1)}, bf16[32,2048]{1,0:T(8,128)(2,1)S(1)}, u32[]{:S(2)}, u32[]{:S(2)}) collective-permute-start(bf16[32,2048]{1,0:T(8,128)(2,1)S(1)} %bitcast.156), channel_id=1, source_target_pairs={{0,2},{2,4},{4,6},{6,8},{8,10},{10,12},{12,14},{14,16},{16,18},{18... | collective-permute-start | bytes 393224 | tf_op jit(solution)/shard_map/ppermute | solution.py:43
  85.9 2.9 %collective-permute-done.8 = bf16[32,2048]{1,0:T(8,128)(2,1)S(1)} collective-permute-done((bf16[32,2048]{1,0:T(8,128)(2,1)S(1)}, bf16[32,2048]{1,0:T(8,128)(2,1)S(1)}, u32[]{:S(2)}, u32[]{:S(2)}) %collective-permute-start.8) | collective-permute-done | bytes 131104 | tf_op jit(solution)/shard_map/ppermute | solution.py:44
  88.8 6.4 %collective-permute-done.7 = bf16[32,2048]{1,0:T(8,128)(2,1)S(1)} collective-permute-done((bf16[32,2048]{1,0:T(8,128)(2,1)S(1)}, bf16[32,2048]{1,0:T(8,128)(2,1)S(1)}, u32[]{:S(2)}, u32[]{:S(2)}) %collective-permute-start.7) | collective-permute-done | bytes 131104 | tf_op jit(solution)/shard_map/ppermute | solution.py:43
  95.3 1.4 %gather_fusion.3 = bf16[32,32,256]{2,1,0:T(8,128)(2,1)} fusion(bf16[32,24,256]{2,0,1:T(8,128)(2,1)S(1)} %pad_maximum_fusion.1, s32[1024]{0:T(1024)S(1)} %pad_clamp_fusion.2), kind=kCustom, calls=%fused_computation.3 | custom fusion | bytes 1048704 | tf_op jit(solution)/shard_map/jit(_take)/gather | solution.py:49
  96.6 1.4 %gather_fusion.4 = bf16[32,32,256]{2,1,0:T(8,128)(2,1)} fusion(bf16[32,24,256]{2,0,1:T(8,128)(2,1)S(1)} %pad_maximum_fusion.1, s32[1024]{0:T(1024)S(1)} %pad_clamp_fusion.1), kind=kCustom, calls=%fused_computation.4 | custom fusion | bytes 1048704 | tf_op jit(solution)/shard_map/jit(_take)/gather | solution.py:49
  98.0 3.7 %convolution_bitcast_fusion.2 = f32[8,32,256]{2,1,0:T(8,128)S(1)} fusion(bf16[32,8,4,256]{3,0,2,1:T(8,128)(2,1)} %bitcast.141, bf16[8,4,256,256]{3,2,1,0:T(8,128)(2,1)} %param.9), kind=kOutput, calls=%fused_computation.14 | convolution fusion | flops 134217728 | bytes 4980736 | tf_op jit(solution)/shard_map/hcsm,cslm->hcl/dot_general | solution.py:50
  101.7 1.2 %fusion.27 = f32[64,32,128]{2,1,0:T(8,128)S(1)} fusion(bf16[64,32,128]{2,1,0:T(8,128)(2,1)S(1)} %bitcast.139, bf16[64,128,128]{2,1,0:T(8,128)(2,1)S(1)} %bitcast.134), kind=kOutput, calls=%fused_computation.59 | convolution fusion | flops 67108864 | bytes 3670016 | tf_op jit(solution)/shard_map/bhm,bkm->bhk/dot_general | solution.py:61
  102.9 1.1 convolution_convert_fusion
  104.4 2.0 %collective-permute-start.9 = (bf16[256,128]{1,0:T(8,128)(2,1)S(1)}, bf16[256,128]{1,0:T(8,128)(2,1)S(1)}, u32[]{:S(2)}, u32[]{:S(2)}) collective-permute-start(bf16[256,128]{1,0:T(8,128)(2,1)S(1)} %get-tuple-element.2), channel_id=1, source_target_pairs={{0,2},{2,4},{4,6},{6,0},{1,3},{3,5},{5,7},{7,1},{8,10},{10,12},{12... | collective-permute-start | bytes 196616 | tf_op jit(solution)/shard_map/ppermute | solution.py:72
  106.4 3.5 %fusion.3 = f32[32,8,256]{2,0,1:T(8,128)S(1)} fusion(f32[8,32,256]{2,1,0:T(8,128)S(1)} %convolution_bitcast_fusion.2, bf16[32,8,4,256]{3,0,2,1:T(8,128)(2,1)S(1)} %bitcast.142, bf16[8,4,256,256]{3,2,1,0:T(8,128)(2,1)} %collective-permute-done.3, bf16[32,8,256]{2,0,1:T(8,128)(2,1)S(1)} %fusion.8), kind=kOutput, calls=%fused_computation.13 | convolution fusion | flops 134479872 | bytes 5373952 | tf_op jit(solution)/shard_map/hcsm,cslm->hcl/dot_general | solution.py:50
  (61 shorter events, 8.1 us)
Async XLA Ops:
  0.6 54.0 %copy-start = (bf16[1,1,32,2,128,128]{5,4,3,2,1,0:T(8,128)(2,1)S(1)}, bf16[1,1,32,2,128,128]{5,4,3,2,1,0:T(8,128)(2,1)}, u32[]{:S(2)}) copy-start(bf16[1,1,32,2,128,128]{5,4,3,2,1,0:T(8,128)(2,1)} %param.11) | copy-start | bytes 6291460
  0.6 66.2 %collective-permute-start.3 = (bf16[8,4,256,256]{3,2,1,0:T(8,128)(2,1)}, bf16[8,4,256,256]{3,2,1,0:T(8,128)(2,1)}, u32[]{:S(2)}, u32[]{:S(2)}) collective-permute-start(bf16[8,4,256,256]{3,2,1,0:T(8,128)(2,1)} %param.9), channel_id=1, source_target_pairs={{0,1},{1,0},{2,3},{3,2},{4,5},{5,4},{6,7},{7,6},{8,9},{9,8},{10,11... | collective-permute-start | bytes 12582920 | tf_op jit(solution)/shard_map/ppermute | solution.py:36
  0.7 39.8 %collective-permute-start = (bf16[32,2048]{1,0:T(8,128)(2,1)}, bf16[32,2048]{1,0:T(8,128)(2,1)S(1)}, u32[]{:S(2)}, u32[]{:S(2)}) collective-permute-start(bf16[32,2048]{1,0:T(8,128)(2,1)} %param.8), channel_id=1, source_target_pairs={{0,2},{2,4},{4,6},{6,8},{8,10},{10,12},{12,14},{14,16},{16,18},{18... | collective-permute-start | bytes 393224 | tf_op jit(solution)/shard_map/ppermute | solution.py:43
  4.4 36.1 %collective-permute-start.1 = (bf16[32,2048]{1,0:T(8,128)(2,1)}, bf16[32,2048]{1,0:T(8,128)(2,1)S(1)}, u32[]{:S(2)}, u32[]{:S(2)}) collective-permute-start(bf16[32,2048]{1,0:T(8,128)(2,1)} %param.8), channel_id=1, source_target_pairs={{2,0},{4,2},{6,4},{8,6},{10,8},{12,10},{14,12},{16,14},{18,16},{20... | collective-permute-start | bytes 393224 | tf_op jit(solution)/shard_map/ppermute | solution.py:44
  12.3 18.4 %all-to-all-start = ((s32[32,1,2]{2,1,0:T(1,128)}), s32[32,1,2]{2,1,0:T(1,128)S(1)}, u32[]{:S(2)}, u32[]{:S(2)}) async-start(s32[32,1,2]{2,1,0:T(1,128)} %copy.51), calls=%async_computation | async-start | bytes 32768 | tf_op jit(solution)/shard_map/all_to_all | solution.py:29
  33.5 21.1 %all-to-all-start.1 = ((bf16[32,64,128]{2,1,0:T(8,128)(2,1)}), bf16[32,64,128]{2,1,0:T(8,128)(2,1)S(1)}, u32[]{:S(2)}, u32[]{:S(2)}) async-start(bf16[32,64,128]{2,1,0:T(8,128)(2,1)} %bitcast.11), calls=%async_computation.1 | async-start | bytes 1048576 | tf_op jit(solution)/shard_map/all_to_all | solution.py:60
  39.2 1.2 %collective-permute-start.2 = (s32[8,4]{0,1:T(4,128)S(1)}, s32[8,4]{0,1:T(4,128)S(1)}, u32[]{:S(2)}, u32[]{:S(2)}) collective-permute-start(s32[8,4]{0,1:T(4,128)S(1)} %broadcast_subtract_fusion), channel_id=1, source_target_pairs={{0,1},{1,0},{2,3},{3,2},{4,5},{5,4},{6,7},{7,6},{8,9},{9,8},{10,11... | collective-permute-start | bytes 392 | tf_op jit(solution)/shard_map/ppermute | solution.py:35
  54.7 7.1 %copy-start.1 = (bf16[8,4,256,256]{3,2,1,0:T(8,128)(2,1)S(1)}, bf16[8,4,256,256]{3,2,1,0:T(8,128)(2,1)}, u32[]{:S(2)}) copy-start(bf16[8,4,256,256]{3,2,1,0:T(8,128)(2,1)} %param.9) | copy-start | bytes 12582916
  55.8 11.0 %copy-start.6 = (bf16[32,2048]{1,0:T(8,128)(2,1)S(1)}, bf16[32,2048]{1,0:T(8,128)(2,1)}, u32[]{:S(2)}) copy-start(bf16[32,2048]{1,0:T(8,128)(2,1)} %param.8) | copy-start | bytes 393220
  57.1 0.7 copy-start.7
  58.5 6.7 %collective-permute-start.4 = (bf16[256,128]{1,0:T(8,128)(2,1)}, bf16[256,128]{1,0:T(8,128)(2,1)}, u32[]{:S(2)}, u32[]{:S(2)}) collective-permute-start(bf16[256,128]{1,0:T(8,128)(2,1)} %get-tuple-element.5), channel_id=1, source_target_pairs={{0,2},{2,4},{4,6},{6,0},{1,3},{3,5},{5,7},{7,1},{8,10},{10,12},{12... | collective-permute-start | bytes 196616 | tf_op jit(solution)/shard_map/ppermute | solution.py:72
  58.5 6.7 %collective-permute-start.5 = (bf16[256,128]{1,0:T(8,128)(2,1)}, bf16[256,128]{1,0:T(8,128)(2,1)}, u32[]{:S(2)}, u32[]{:S(2)}) collective-permute-start(bf16[256,128]{1,0:T(8,128)(2,1)} %get-tuple-element.7), channel_id=1, source_target_pairs={{0,4},{2,6},{4,0},{6,2},{1,5},{3,7},{5,1},{7,3},{8,12},{10,14},{12... | collective-permute-start | bytes 196616 | tf_op jit(solution)/shard_map/ppermute | solution.py:72
  60.0 5.8 %collective-permute-start.6 = (bf16[256,128]{1,0:T(8,128)(2,1)}, bf16[256,128]{1,0:T(8,128)(2,1)}, u32[]{:S(2)}, u32[]{:S(2)}) collective-permute-start(bf16[256,128]{1,0:T(8,128)(2,1)} %get-tuple-element.6), channel_id=1, source_target_pairs={{0,6},{2,0},{4,2},{6,4},{1,7},{3,1},{5,3},{7,5},{8,14},{10,8},{12,... | collective-permute-start | bytes 196616 | tf_op jit(solution)/shard_map/ppermute | solution.py:72
  63.8 7.1 %copy-start.2 = (bf16[8,256,128]{2,1,0:T(8,128)(2,1)S(1)}, bf16[8,256,128]{2,1,0:T(8,128)(2,1)}, u32[]{:S(2)}) copy-start(bf16[8,256,128]{2,1,0:T(8,128)(2,1)} %param.15) | copy-start | bytes 1572868
  65.1 5.4 %copy-start.3 = (bf16[8,256,128]{2,1,0:T(8,128)(2,1)S(1)}, bf16[8,256,128]{2,1,0:T(8,128)(2,1)}, u32[]{:S(2)}) copy-start(bf16[8,256,128]{2,1,0:T(8,128)(2,1)} %param.14) | copy-start | bytes 1572868
  72.5 29.2 %all-to-all-start.2 = ((bf16[32,64,128]{2,1,0:T(8,128)(2,1)}), bf16[32,64,128]{2,1,0:T(8,128)(2,1)S(1)}, u32[]{:S(2)}, u32[]{:S(2)}) async-start(bf16[32,64,128]{2,1,0:T(8,128)(2,1)} %bitcast.30), calls=%async_computation.2 | async-start | bytes 1048576 | tf_op jit(solution)/shard_map/all_to_all | solution.py:60
  77.6 17.6 %copy-start.8 = (bf16[8,4,8,256]{3,2,0,1:T(8,128)(2,1)}, bf16[8,4,8,256]{3,2,0,1:T(8,128)(2,1)S(1)}, u32[]{:S(2)}) copy-start(bf16[8,4,8,256]{3,2,0,1:T(8,128)(2,1)S(1)} %copy.68) | copy-start | bytes 393220
  77.6 11.2 %collective-permute-start.8 = (bf16[32,2048]{1,0:T(8,128)(2,1)S(1)}, bf16[32,2048]{1,0:T(8,128)(2,1)S(1)}, u32[]{:S(2)}, u32[]{:S(2)}) collective-permute-start(bf16[32,2048]{1,0:T(8,128)(2,1)S(1)} %bitcast.155), channel_id=1, source_target_pairs={{2,0},{4,2},{6,4},{8,6},{10,8},{12,10},{14,12},{16,14},{18,16},{20... | collective-permute-start | bytes 393224 | tf_op jit(solution)/shard_map/ppermute | solution.py:44
  84.0 11.2 %collective-permute-start.7 = (bf16[32,2048]{1,0:T(8,128)(2,1)S(1)}, bf16[32,2048]{1,0:T(8,128)(2,1)S(1)}, u32[]{:S(2)}, u32[]{:S(2)}) collective-permute-start(bf16[32,2048]{1,0:T(8,128)(2,1)S(1)} %bitcast.156), channel_id=1, source_target_pairs={{0,2},{2,4},{4,6},{6,8},{8,10},{10,12},{12,14},{14,16},{16,18},{18... | collective-permute-start | bytes 393224 | tf_op jit(solution)/shard_map/ppermute | solution.py:43
  101.7 4.7 %copy-start.5 = (bf16[32,32,256]{2,1,0:T(8,128)(2,1)S(1)}, bf16[32,32,256]{2,1,0:T(8,128)(2,1)}, u32[]{:S(2)}) copy-start(bf16[32,32,256]{2,1,0:T(8,128)(2,1)} %gather_fusion.4) | copy-start | bytes 1572868
  102.9 7.9 %copy-start.4 = (bf16[8,256,128]{2,1,0:T(8,128)(2,1)S(1)}, bf16[8,256,128]{2,1,0:T(8,128)(2,1)}, u32[]{:S(2)}) copy-start(bf16[8,256,128]{2,1,0:T(8,128)(2,1)} %param.14) | copy-start | bytes 1572868
  104.2 5.9 %collective-permute-start.10 = (bf16[256,128]{1,0:T(8,128)(2,1)S(1)}, bf16[256,128]{1,0:T(8,128)(2,1)S(1)}, u32[]{:S(2)}, u32[]{:S(2)}) collective-permute-start(bf16[256,128]{1,0:T(8,128)(2,1)S(1)} %get-tuple-element.4), channel_id=1, source_target_pairs={{0,4},{2,6},{4,0},{6,2},{1,5},{3,7},{5,1},{7,3},{8,12},{10,14},{12... | collective-permute-start | bytes 196616 | tf_op jit(solution)/shard_map/ppermute | solution.py:72
  104.3 5.8 %collective-permute-start.11 = (bf16[256,128]{1,0:T(8,128)(2,1)S(1)}, bf16[256,128]{1,0:T(8,128)(2,1)S(1)}, u32[]{:S(2)}, u32[]{:S(2)}) collective-permute-start(bf16[256,128]{1,0:T(8,128)(2,1)S(1)} %get-tuple-element.3), channel_id=1, source_target_pairs={{0,6},{2,0},{4,2},{6,4},{1,7},{3,1},{5,3},{7,5},{8,14},{10,8},{12,... | collective-permute-start | bytes 196616 | tf_op jit(solution)/shard_map/ppermute | solution.py:72
  104.4 6.4 %collective-permute-start.9 = (bf16[256,128]{1,0:T(8,128)(2,1)S(1)}, bf16[256,128]{1,0:T(8,128)(2,1)S(1)}, u32[]{:S(2)}, u32[]{:S(2)}) collective-permute-start(bf16[256,128]{1,0:T(8,128)(2,1)S(1)} %get-tuple-element.2), channel_id=1, source_target_pairs={{0,2},{2,4},{4,6},{6,0},{1,3},{3,5},{5,7},{7,1},{8,10},{10,12},{12... | collective-permute-start | bytes 196616 | tf_op jit(solution)/shard_map/ppermute | solution.py:72

commit v2 on v1

v2 whole, which is shorter than its diff:
```python
import functools

import jax
import jax.numpy as jnp
from jax import lax
from jax.experimental import pallas as pl
from jax.experimental.pallas import tpu as pltpu
from jax.sharding import PartitionSpec as P

SMEM = pl.BlockSpec(memory_space=pltpu.SMEM)
VMEM = pl.BlockSpec(memory_space=pltpu.VMEM)
HBM = pl.BlockSpec(memory_space=pltpu.HBM)
NN = (((1,), (0,)), ((), ()))
NT = (((1,), (1,)), ((), ()))


def in_hbm(x):
    return pltpu.with_memory_space_constraint(x, pltpu.HBM)


def pinned(x):
    return pltpu.with_memory_space_constraint(x, pltpu.VMEM)


def product(a, b, dims=NT):
    return lax.dot_general(a, b, dims, preferred_element_type=jnp.float32)


def params(mib):
    return pltpu.CompilerParams(vmem_limit_bytes=mib * 2**20)


def cost(flops, moved):
    return pl.CostEstimate(flops=flops, bytes_accessed=moved, transcendentals=0)


def stage_kernel(*refs):
    count = (len(refs) - 1) // 3
    sources, turned, held = (refs[k * count : (k + 1) * count] for k in range(3))
    sems = refs[-1]
    copies = []
    for source, hold in zip(sources, held):
        for k in range(source.shape[0]):
            sem = sems.at[len(copies)]
            copies.append(pltpu.make_async_copy(source.at[k], hold.at[k], sem))
    for copy in copies:
        copy.start()
    at = 0
    for source, out, hold in zip(sources, turned, held):
        for k in range(source.shape[0]):
            copies[at].wait()
            at += 1
            for n in range(source.shape[1]):
                out[k, n] = hold[k, n].T


def stage(*arrays):
    size = sum(x.size * x.dtype.itemsize for x in arrays)
    return pl.pallas_call(
        stage_kernel,
        out_shape=[pltpu.VMEM(x.shape, x.dtype) for x in arrays],
        in_specs=[HBM] * len(arrays),
        out_specs=[VMEM] * len(arrays),
        scratch_shapes=[pltpu.VMEM(x.shape, x.dtype) for x in arrays]
        + [pltpu.SemaphoreType.DMA((sum(x.shape[0] for x in arrays),))],
        compiler_params=params(20),
        cost_estimate=cost(0, 2 * size),
        name="stage",
    )(*[pltpu.with_memory_space_constraint(x, pltpu.HBM) for x in arrays])


def pick_into(wanted_ref, coeffs_ref, packed_ref):
    peers, slots = wanted_ref.shape[0], wanted_ref.shape[2]
    batch = 8
    for at in range(0, peers * slots, batch):
        taken = [
            coeffs_ref[wanted_ref[b // slots, 0, b % slots]] for b in range(at, at + batch)
        ]
        for k, block in enumerate(taken):
            packed_ref[at + k] = block


def pick(wanted, coeffs):
    pairs = wanted.shape[0] * wanted.shape[2]
    return pl.pallas_call(
        pick_into,
        out_shape=pltpu.VMEM((pairs, *coeffs.shape[1:]), coeffs.dtype),
        in_specs=[SMEM, VMEM],
        out_specs=VMEM,
        compiler_params=params(4),
        cost_estimate=cost(0, 600_000),
        name="pick",
    )(wanted, coeffs)


def couple_kernel(place_ref, target_ref, picked_ref, couple_ref, own_ref, *rest):
    parts, total = rest[:-1], rest[-1]
    clusters = own_ref.shape[0]
    peers = len(parts) + 1
    total[...] = jnp.zeros_like(total)
    slots = target_ref.shape[0]
    for b in range(picked_ref.shape[0]):
        row = target_ref[b % slots, b // slots]
        block = couple_ref[b // slots, b % slots]
        total[row] = total[row] + product(picked_ref[b], block, NN)
    place = place_ref[0]
    own_ref[...] = total[pl.ds(place * clusters, clusters)]
    for step, part in enumerate(parts, 1):
        at = lax.rem(place + step, peers) * clusters
        part[...] = total[pl.ds(at, clusters)].astype(part.dtype)


def couple_and_add(place, targets, picked, couple, clusters, peers):
    pairs, cols, rank = picked.shape
    part = jax.ShapeDtypeStruct((clusters, cols, rank), picked.dtype)
    return pl.pallas_call(
        couple_kernel,
        out_shape=[jax.ShapeDtypeStruct(part.shape, jnp.float32)] + [part] * (peers - 1),
        in_specs=[SMEM, SMEM, VMEM, VMEM],
        out_specs=[VMEM] * peers,
        scratch_shapes=[pltpu.VMEM((clusters * peers, cols, rank), jnp.float32)],
        compiler_params=params(8),
        cost_estimate=cost(2 * pairs * cols * rank * rank, 4_000_000),
        name="couple",
    )(place, targets, picked, pinned(couple))


def near_kernel(
    first_ref, here, there, before, current, after, a_ref, b_ref, out_ref,
    window, a_held, b_held, turned, sems,
):
    clusters, slots, leaf = a_ref.shape[0], a_ref.shape[1], a_ref.shape[2]
    width = current.shape[1]
    copies = []
    for c in range(clusters):
        for source, held in ((a_ref, a_held), (b_ref, b_held)):
            copies.append(
                pltpu.make_async_copy(source.at[c], held.at[c], sems.at[len(copies)])
            )
    for copy in copies:
        copy.start()
    for k, piece in enumerate((before, current, after)):
        window[:, k * width : (k + 1) * width] = piece[...]
    first = first_ref[0]
    for c in range(clusters):
        total = 0.5 * current[:, c * leaf : (c + 1) * leaf].astype(jnp.float32)
        for k, (cols, held) in enumerate(((here, a_held), (there, b_held))):
            copies[2 * c + k].wait()
            for s in range(slots):
                block = turned.at[c % 2, k * slots + s]
                block[...] = held[c, s].T
                start = pl.multiple_of((cols[s, c] - first) * leaf, leaf)
                total = total + product(window[:, pl.ds(start, leaf)], block[...], NN)
        out_ref[c] = total


def near_terms(first, here, there, before, current, after, a, b):
    clusters, slots, leaf, _ = a.shape
    cols, width = current.shape
    return pl.pallas_call(
        near_kernel,
        out_shape=jax.ShapeDtypeStruct((clusters, cols, leaf), jnp.float32),
        in_specs=[SMEM] * 3 + [VMEM] * 3 + [HBM] * 2,
        out_specs=VMEM,
        scratch_shapes=[
            pltpu.VMEM((cols, 3 * width), current.dtype),
            pltpu.VMEM(a.shape, a.dtype),
            pltpu.VMEM(b.shape, b.dtype),
            pltpu.VMEM((2, 2 * slots, leaf, leaf), a.dtype),
            pltpu.SemaphoreType.DMA((2 * clusters,)),
        ],
        compiler_params=params(16),
        cost_estimate=cost(4 * clusters * slots * cols * leaf * leaf, 9_000_000),
        name="near",
    )(first, here, there, before, current, after, in_hbm(a), in_hbm(b))


def image_into(c, own, parts, row_basis, near, image):
    leaf = row_basis.shape[1]
    total = own[c]
    for part in parts:
        total = total + part[c].astype(jnp.float32)
    coupled = total.astype(image.dtype)
    at = slice(c * leaf, (c + 1) * leaf)
    value = near[c] + product(coupled, row_basis[c])
    value = value.astype(image.dtype)
    image[:, at] = value
    return value


def last_kernel(own, *refs):
    *parts, row_basis, near, image = refs
    for c in range(own.shape[0]):
        image_into(c, own, parts, row_basis, near, image)


def middle_kernel(wanted_ref, own, *refs):
    *parts, row_basis, near, column_basis, image, packed, coeffs = refs
    for c in range(own.shape[0]):
        value = image_into(c, own, parts, row_basis, near, image)
        coeffs[c] = product(value, column_basis[c], NN).astype(coeffs.dtype)
    pick_into(wanted_ref, coeffs, packed)


def finish(own, parts, row_basis, near):
    clusters, cols, _ = own.shape
    dtype = row_basis.dtype
    return pl.pallas_call(
        last_kernel,
        out_shape=jax.ShapeDtypeStruct((cols, clusters * row_basis.shape[1]), dtype),
        in_specs=[VMEM] * (len(parts) + 3),
        out_specs=VMEM,
        compiler_params=params(8),
        cost_estimate=cost(20_000_000, 1_500_000),
        name="finish",
    )(own, *parts, row_basis, near)


def finish_and_pick(wanted, own, parts, row_basis, near, column_basis):
    clusters, cols, rank = own.shape
    pairs = wanted.shape[0] * wanted.shape[2]
    dtype = row_basis.dtype
    return pl.pallas_call(
        middle_kernel,
        out_shape=[
            jax.ShapeDtypeStruct((cols, clusters * row_basis.shape[1]), dtype),
            jax.ShapeDtypeStruct((pairs, cols, rank), dtype),
        ],
        in_specs=[SMEM] + [VMEM] * (len(parts) + 4),
        out_specs=[VMEM, VMEM],
        scratch_shapes=[pltpu.VMEM((clusters, cols, rank), dtype)],
        compiler_params=params(8),
        cost_estimate=cost(40_000_000, 2_500_000),
        name="finish_and_pick",
    )(wanted, own, *parts, row_basis, near, column_basis)


def per_device(
    vector,
    near_blocks,
    near_cols,
    coupling,
    far_dst,
    far_src,
    row_cluster_basis,
    column_cluster_basis,
):
    clusters, leaf_size, basis_rank = row_cluster_basis.shape
    row_peers = lax.axis_size("row")
    col_peers = lax.axis_size("col")
    slot_count = far_src.shape[3]
    pairs = row_peers * slot_count
    own_cols = vector.shape[0]
    wanted = lax.all_to_all(far_src.reshape(row_peers, 1, slot_count), "row", 0, 0, tiled=True)

    other = [(0, 1), (1, 0)]
    first = ((lax.axis_index(("row", "col")) - 1) * clusters).astype(jnp.int32).reshape(1)
    our_cols = near_cols.T
    their_cols = lax.ppermute(our_cols, "rhs", other)
    targets = far_dst.reshape(row_peers, slot_count).T
    place = lax.axis_index("col").astype(jnp.int32).reshape(1)
    line = row_peers * col_peers
    up = [(i, i + 1) for i in range(line - 1)]
    down = [(j, i) for i, j in up]

    leaves = vector.reshape(own_cols, clusters, leaf_size)
    coeffs = jnp.einsum(
        "sao,aon->asn", leaves, column_cluster_basis, preferred_element_type=jnp.float32
    ).astype(jnp.bfloat16)
    couple = stage(coupling.reshape(row_peers, slot_count, basis_rank, basis_rank))[0]
    theirs = lax.ppermute(near_blocks, "rhs", other)
    wanted, their_cols = lax.optimization_barrier((wanted, their_cols))
    packed = pick(wanted, coeffs)

    def exchanges(current, packed):
        packed, current = lax.optimization_barrier((packed, current))
        before = lax.ppermute(current, ("row", "col"), up)
        after = lax.ppermute(current, ("row", "col"), down)
        blocks = packed.reshape(row_peers, slot_count * own_cols, basis_rank)
        picked = lax.all_to_all(blocks, "row", 0, 0, tiled=True)
        picked = picked.reshape(pairs, own_cols, basis_rank)
        own, *parts = couple_and_add(place, targets, picked, couple, clusters, col_peers)
        near = near_terms(
            first, our_cols, their_cols, before, current, after, near_blocks, theirs
        )
        moved = []
        for step, part in enumerate(parts, 1):
            ring = [(i, (i + step) % col_peers) for i in range(col_peers)]
            moved.append(lax.ppermute(part, "col", ring))
        return own, moved, near

    own, parts, near = exchanges(vector, packed)
    first_image, packed = finish_and_pick(
        wanted, own, parts, row_cluster_basis, near, column_cluster_basis
    )
    own, parts, near = exchanges(first_image, packed)
    second_image = finish(own, parts, row_cluster_basis, near)
    return (first_image, second_image)


def solution(mesh):
    return jax.shard_map(
        per_device,
        mesh=mesh,
        in_specs=(
            P("rhs", ("row", "col")),
            P(("row", "col"), "rhs", None, None),
            P(("row", "col"), "rhs"),
            P("row", "col", None, None, None, None),
            P("row", "col", None, None),
            P("row", "col", None, None),
            P(("row", "col"), None, None),
            P(("row", "col"), None, None),
        ),
        out_specs=(P("rhs", ("row", "col")), P("rhs", ("row", "col"))),
        check_vma=False,
    )
```

time: 112 us -> 96.8 us (0.86)
  Pallas kernels: 0 us -> 23.5 us
  matrix products: 19.6 us -> 1.32 us
  waiting for transfers between devices: 30.5 us -> 20 us
  local copies, waits for them, and re-layouts: 13.2 us -> 3.1 us
  starting transfers between devices: 44.1 us -> 47.5 us
  other arithmetic: 3.39 us -> 0 us
    pallas_call x0 -> x8, Pallas kernels: none -> 23.5 us  [the longest x2 11.7 us: near_terms(): pl.pallas_call(near_kernel, out_shape=jax.ShapeDtypeStruct((clusters, col...]
    dot_general x12 -> x1, matrix products: 19.6 us -> 1.32 us  [per_device(): jnp.einsum('sao,aon->asn', leaves, column_cluster_basis, preferred_elemen...]
    ppermute x12, waiting for transfers between devices: 10.8 us -> 0.03 us  [the longest x6 0.02 us: exchanges(): moved.append(lax.ppermute(part, 'col', ring))]
    gather x6 -> x0, local copies, waits for them, and re-layouts: 7.59 us -> none  [the longest x4 4.73 us: near_of(): taken = jnp.take(window, cols, axis=1, mode='clip')]
    ppermute x12, starting transfers between devices: 24 us -> 26.1 us  [the longest x2 11.6 us: exchanges(): after = lax.ppermute(current, ('row', 'col'), down)]
    all_to_all x2 -> x0, local copies, waits for them, and re-layouts: 1.88 us -> none  [per_device(): wanted = lax.all_to_all(far_src.reshape(row_peers, slot_count), 'row', 0, 0)]
    all_to_all x3, starting transfers between devices: 20 us -> 21.4 us  [the longest x1 11.2 us: per_device(): lax.all_to_all(far_src.reshape(row_peers, 1, slot_count), 'row', 0, 0, ti...]
  transfers between devices with their start and end apart: 15 -> 15, of which waited for: 8 -> 3; matrix products, arithmetic and copies ran while one was open for 24% -> 3% of each run, Pallas kernels for 0% -> 21%
where the time goes in v2:
time: 96.8 us; the launch traced here: 96.3 us
  starting transfers between devices  47.5 us (49%)
  Pallas kernels  23.5 us (24%)
  waiting for transfers between devices  20 us (21%)
  local copies, waits for them, and re-layouts  3.1 us (3%)
  matrix products  1.32 us (1%)
    all_to_all x2, waiting for transfers between devices, exchanges(): picked = lax.all_to_all(blocks, 'row', 0, 0, tiled=True)  12.8 us
    pallas_call x2, Pallas kernels, near_terms(): pl.pallas_call(near_kernel, out_shape=jax.ShapeDtypeStruct((clusters, col...  11.7 us
    ppermute x2, starting transfers between devices, exchanges(): after = lax.ppermute(current, ('row', 'col'), down)  11.6 us
    all_to_all x1, starting transfers between devices, per_device(): lax.all_to_all(far_src.reshape(row_peers, 1, slot_count), 'row', 0, 0, ti...  11.2 us
    all_to_all x2, starting transfers between devices, exchanges(): picked = lax.all_to_all(blocks, 'row', 0, 0, tiled=True)  10.2 us
    ppermute x6, starting transfers between devices, exchanges(): moved.append(lax.ppermute(part, 'col', ring))  10.1 us
    all_to_all x1, waiting for transfers between devices, per_device(): lax.all_to_all(far_src.reshape(row_peers, 1, slot_count), 'row', 0, 0, ti...  7.16 us
    ppermute x2, starting transfers between devices, exchanges(): before = lax.ppermute(current, ('row', 'col'), up)  3.84 us
  transfers between devices with their start and end apart: 15, of which 3 were waited for; matrix products, arithmetic and copies ran while one was open for 3% of the time, Pallas kernels for 21%

profile of v2, /device:TPU:32, one launch (start us, length us, event | category | flops | bytes accessed | tf_op | source)
XLA Modules:
  0.0 96.3 jit_solution(13057606190508443101)
XLA Ops:
  0.6 0.1 collective-permute-start.6
  0.7 0.5 collective-permute-start
  1.2 1.4 %copy.10 = s32[32,1,2]{2,1,0:T(1,128)} copy(s32[32,1,2]{0,2,1:T(2,128)} %bitcast.27) | data formatting | bytes 512 | tf_op jit(solution)/shard_map/reshape | solution.py:254
  2.6 11.2 %all-to-all-start = ((s32[32,1,2]{2,1,0:T(1,128)}), s32[32,1,2]{2,1,0:T(1,128)S(1)}, u32[]{:S(2)}, u32[]{:S(2)}) async-start(s32[32,1,2]{2,1,0:T(1,128)} %copy.10), calls=%async_computation | async-start | bytes 32768 | tf_op jit(solution)/shard_map/all_to_all | solution.py:254
  13.8 1.3 %convolution_convert_fusion.coeffs_ref = bf16[8,32,128]{2,1,0:T(8,128)(2,1)S(1)} fusion(bf16[8,256,128]{2,1,0:T(8,128)(2,1)} %refs_5_.1, bf16[4,8,8,256]{3,2,1,0:T(8,128)(2,1)} %bitcast.19), kind=kOutput, calls=%fused_computation | convolution fusion | flops 16809984 | bytes 720896 | tf_op jit(solution)/shard_map/sao,aon->asn/dot_general | solution.py:267
  15.1 0.0 copy-start.2
  15.1 0.0 copy-start.5
  15.2 7.2 %all-to-all-done.wanted_ref = s32[32,1,2]{2,1,0:T(1,128)S(1)} async-done(((s32[32,1,2]{2,1,0:T(1,128)}), s32[32,1,2]{2,1,0:T(1,128)S(1)}, u32[]{:S(2)}, u32[]{:S(2)}) %all-to-all-start) | async-done | bytes 288 | tf_op jit(solution)/shard_map/all_to_all | solution.py:254
  22.3 1.7 %pick.1 = bf16[64,32,128]{2,1,0:T(8,128)(2,1)} custom-call(s32[32,1,2]{2,1,0:T(1,128)S(1)} %all-to-all-done.wanted_ref, bf16[8,32,128]{2,1,0:T(8,128)(2,1)S(1)} %convolution_convert_fusion.coeffs_ref), custom_call_target="tpu_custom_call" | custom-call | bytes 600000 | tf_op jit(solution)/shard_map/pick/pallas_call | solution.py:85
  24.0 4.9 %all-to-all-start.1 = ((bf16[32,64,128]{2,1,0:T(8,128)(2,1)}), bf16[32,64,128]{2,1,0:T(8,128)(2,1)S(1)}, u32[]{:S(2)}, u32[]{:S(2)}) async-start(bf16[32,64,128]{2,1,0:T(8,128)(2,1)} %bitcast.5), calls=%async_computation.1 | async-start | bytes 1048576 | tf_op jit(solution)/shard_map/all_to_all | solution.py:280
  28.9 7.0 %collective-permute-start.5 = (bf16[32,2048]{1,0:T(8,128)(2,1)}, bf16[32,2048]{1,0:T(8,128)(2,1)S(1)}, u32[]{:S(2)}, u32[]{:S(2)}) collective-permute-start(bf16[32,2048]{1,0:T(8,128)(2,1)} %current), channel_id=1, source_target_pairs={{2,0},{4,2},{6,4},{8,6},{10,8},{12,10},{14,12},{16,14},{18,16},{20... | collective-permute-start | bytes 393224 | tf_op jit(solution)/shard_map/ppermute | solution.py:278
  35.9 1.9 %collective-permute-start.4 = (bf16[32,2048]{1,0:T(8,128)(2,1)}, bf16[32,2048]{1,0:T(8,128)(2,1)S(1)}, u32[]{:S(2)}, u32[]{:S(2)}) collective-permute-start(bf16[32,2048]{1,0:T(8,128)(2,1)} %current), channel_id=1, source_target_pairs={{0,2},{2,4},{4,6},{6,8},{8,10},{10,12},{12,14},{14,16},{16,18},{18... | collective-permute-start | bytes 393224 | tf_op jit(solution)/shard_map/ppermute | solution.py:277
  37.9 3.4 %stage.1.couple_ref = bf16[32,2,128,128]{3,2,1,0:T(8,128)(2,1)S(1)} custom-call(bf16[32,2,128,128]{3,2,1,0:T(8,128)(2,1)} %bitcast.26), custom_call_target="tpu_custom_call" | custom-call | bytes 4194304 | tf_op jit(solution)/shard_map/stage/pallas_call | solution.py:59
  41.3 4.1 %all-to-all-done.1 = bf16[32,64,128]{2,1,0:T(8,128)(2,1)S(1)} async-done(((bf16[32,64,128]{2,1,0:T(8,128)(2,1)}), bf16[32,64,128]{2,1,0:T(8,128)(2,1)S(1)}, u32[]{:S(2)}, u32[]{:S(2)}) %all-to-all-start.1) | async-done | bytes 524320 | tf_op jit(solution)/shard_map/all_to_all | solution.py:280
  45.4 1.9 %couple.2 = (f32[8,32,128]{2,1,0:T(8,128)S(1)}, bf16[8,32,128]{2,1,0:T(8,128)(2,1)}, bf16[8,32,128]{2,1,0:T(8,128)(2,1)S(1)}, bf16[8,32,128]{2,1,0:T(8,128)(2,1)S(1)}) custom-call(s32[1]{0:T(128)} %bitcast.2.place_ref, s32[2,32]{1,0:T(2,128)S(1)} %bitcast.24, bf16[64,32,128]{2,1,0:T(8,128)(2,1)S(1)} %bitcast.17, bf16[32,2,128,128]{3,2,1,0:T(8,128)(2,1)S(1)} %stage.1.couple_ref), custom_call_target="tpu_custom_call" | custom-call | flops 67108864 | bytes 4000000 | tf_op jit(solution)/shard_map/couple/pallas_call | solution.py:116
  47.3 1.6 %collective-permute-start.1 = (bf16[8,32,128]{2,1,0:T(8,128)(2,1)}, bf16[8,32,128]{2,1,0:T(8,128)(2,1)S(1)}, u32[]{:S(2)}, u32[]{:S(2)}) collective-permute-start(bf16[8,32,128]{2,1,0:T(8,128)(2,1)} %get-tuple-element.21), channel_id=1, source_target_pairs={{0,2},{2,4},{4,6},{6,0},{1,3},{3,5},{5,7},{7,1},{8,10},{10,12},{12... | collective-permute-start | bytes 196616 | tf_op jit(solution)/shard_map/ppermute | solution.py:289
  48.8 2.9 %collective-permute-start.2 = (bf16[8,32,128]{2,1,0:T(8,128)(2,1)S(1)}, bf16[8,32,128]{2,1,0:T(8,128)(2,1)S(1)}, u32[]{:S(2)}, u32[]{:S(2)}) collective-permute-start(bf16[8,32,128]{2,1,0:T(8,128)(2,1)S(1)} %get-tuple-element.22), channel_id=1, source_target_pairs={{0,4},{2,6},{4,0},{6,2},{1,5},{3,7},{5,1},{7,3},{8,12},{10,14},{12... | collective-permute-start | bytes 196616 | tf_op jit(solution)/shard_map/ppermute | solution.py:289
  51.7 1.4 %collective-permute-start.3 = (bf16[8,32,128]{2,1,0:T(8,128)(2,1)S(1)}, bf16[8,32,128]{2,1,0:T(8,128)(2,1)S(1)}, u32[]{:S(2)}, u32[]{:S(2)}) collective-permute-start(bf16[8,32,128]{2,1,0:T(8,128)(2,1)S(1)} %get-tuple-element.23), channel_id=1, source_target_pairs={{0,6},{2,0},{4,2},{6,4},{1,7},{3,1},{5,3},{7,5},{8,14},{10,8},{12,... | collective-permute-start | bytes 196616 | tf_op jit(solution)/shard_map/ppermute | solution.py:289
  53.1 5.8 %near.2.refs_4_ = f32[8,32,256]{2,1,0:T(8,128)S(1)} custom-call(s32[1]{0:T(128)} %bitcast.8.first_ref, s32[4,8]{1,0:T(4,128)S(1)} %bitcast.22, s32[4,8]{1,0:T(4,128)S(1)} %collective-permute-done.there, bf16[32,2048]{1,0:T(8,128)(2,1)S(1)} %collective-permute-done.4.before, bf16[32,2048]{1,0:T(8,128)(2,1)S(1)} %copy-done.2, ...), custom_call_target="tpu_custom_call" | custom-call | flops 268435456 | bytes 9000000 | tf_op jit(solution)/shard_map/near/pallas_call | solution.py:160
  59.0 2.7 %finish_and_pick.1 = (bf16[32,2048]{1,0:T(8,128)(2,1)}, bf16[64,32,128]{2,1,0:T(8,128)(2,1)S(1)}) custom-call(s32[32,1,2]{2,1,0:T(1,128)S(1)} %all-to-all-done.wanted_ref, f32[8,32,128]{2,1,0:T(8,128)S(1)} %get-tuple-element.20.own, bf16[8,32,128]{2,1,0:T(8,128)(2,1)S(1)} %collective-permute-done.1.refs_0_, ...), custom_call_target="tpu_custom_call" | custom-call | flops 40000000 | bytes 2500000 | tf_op jit(solution)/shard_map/finish_and_pick/pallas_call | solution.py:223
  61.7 0.8 copy-done.3
  62.5 5.3 %all-to-all-start.2 = ((bf16[32,64,128]{2,1,0:T(8,128)(2,1)}), bf16[32,64,128]{2,1,0:T(8,128)(2,1)S(1)}, u32[]{:S(2)}, u32[]{:S(2)}) async-start(bf16[32,64,128]{2,1,0:T(8,128)(2,1)} %bitcast.20), calls=%async_computation.2 | async-start | bytes 1048576 | tf_op jit(solution)/shard_map/all_to_all | solution.py:280
  67.8 4.6 %collective-permute-start.11 = (bf16[32,2048]{1,0:T(8,128)(2,1)}, bf16[32,2048]{1,0:T(8,128)(2,1)S(1)}, u32[]{:S(2)}, u32[]{:S(2)}) collective-permute-start(bf16[32,2048]{1,0:T(8,128)(2,1)} %get-tuple-element.33.current), channel_id=1, source_target_pairs={{2,0},{4,2},{6,4},{8,6},{10,8},{12,10},{14,12},{16,14},{18,16},{20... | collective-permute-start | bytes 393224 | tf_op jit(solution)/shard_map/ppermute | solution.py:278
  72.4 1.9 %collective-permute-start.10 = (bf16[32,2048]{1,0:T(8,128)(2,1)}, bf16[32,2048]{1,0:T(8,128)(2,1)S(1)}, u32[]{:S(2)}, u32[]{:S(2)}) collective-permute-start(bf16[32,2048]{1,0:T(8,128)(2,1)} %get-tuple-element.33.current), channel_id=1, source_target_pairs={{0,2},{2,4},{4,6},{6,8},{8,10},{10,12},{12,14},{14,16},{16,18},{18... | collective-permute-start | bytes 393224 | tf_op jit(solution)/shard_map/ppermute | solution.py:277
  74.4 8.7 %all-to-all-done.2 = bf16[32,64,128]{2,1,0:T(8,128)(2,1)S(1)} async-done(((bf16[32,64,128]{2,1,0:T(8,128)(2,1)}), bf16[32,64,128]{2,1,0:T(8,128)(2,1)S(1)}, u32[]{:S(2)}, u32[]{:S(2)}) %all-to-all-start.2) | async-done | bytes 524320 | tf_op jit(solution)/shard_map/all_to_all | solution.py:280
  83.1 1.2 %couple.3 = (f32[8,32,128]{2,1,0:T(8,128)S(1)}, bf16[8,32,128]{2,1,0:T(8,128)(2,1)S(1)}, bf16[8,32,128]{2,1,0:T(8,128)(2,1)S(1)}, bf16[8,32,128]{2,1,0:T(8,128)(2,1)S(1)}) custom-call(s32[1]{0:T(128)} %bitcast.2.place_ref, s32[2,32]{1,0:T(2,128)S(1)} %bitcast.25, bf16[64,32,128]{2,1,0:T(8,128)(2,1)S(1)} %bitcast.18, ...), custom_call_target="tpu_custom_call" | custom-call | flops 67108864 | bytes 4000000 | tf_op jit(solution)/shard_map/couple/pallas_call | solution.py:116
  84.3 1.3 %collective-permute-start.7 = (bf16[8,32,128]{2,1,0:T(8,128)(2,1)S(1)}, bf16[8,32,128]{2,1,0:T(8,128)(2,1)S(1)}, u32[]{:S(2)}, u32[]{:S(2)}) collective-permute-start(bf16[8,32,128]{2,1,0:T(8,128)(2,1)S(1)} %get-tuple-element.30), channel_id=1, source_target_pairs={{0,2},{2,4},{4,6},{6,0},{1,3},{3,5},{5,7},{7,1},{8,10},{10,12},{12... | collective-permute-start | bytes 196616 | tf_op jit(solution)/shard_map/ppermute | solution.py:289
  85.6 0.6 collective-permute-start.8
  86.3 2.3 %collective-permute-start.9 = (bf16[8,32,128]{2,1,0:T(8,128)(2,1)S(1)}, bf16[8,32,128]{2,1,0:T(8,128)(2,1)S(1)}, u32[]{:S(2)}, u32[]{:S(2)}) collective-permute-start(bf16[8,32,128]{2,1,0:T(8,128)(2,1)S(1)} %get-tuple-element.32), channel_id=1, source_target_pairs={{0,6},{2,0},{4,2},{6,4},{1,7},{3,1},{5,3},{7,5},{8,14},{10,8},{12,... | collective-permute-start | bytes 196616 | tf_op jit(solution)/shard_map/ppermute | solution.py:289
  88.6 0.9 copy-done.4
  89.5 5.8 %near.3.refs_4_ = f32[8,32,256]{2,1,0:T(8,128)S(1)} custom-call(s32[1]{0:T(128)} %bitcast.8.first_ref, s32[4,8]{1,0:T(4,128)S(1)} %bitcast.23, s32[4,8]{1,0:T(4,128)S(1)} %collective-permute-done.there, bf16[32,2048]{1,0:T(8,128)(2,1)S(1)} %collective-permute-done.10.before, bf16[32,2048]{1,0:T(8,128)(2,1)S(1)} %copy-done.4, ...), custom_call_target="tpu_custom_call" | custom-call | flops 268435456 | bytes 9000000 | tf_op jit(solution)/shard_map/near/pallas_call | solution.py:160
  95.4 0.9 finish.1
  (22 shorter events, 0.1 us)
Async XLA Ops:
  0.6 44.8 %copy-start.6 = (s32[1,1,32,2]{2,3,1,0:T(2,128)S(1)}, s32[1,1,32,2]{2,3,1,0:T(2,128)}, u32[]{:S(2)}) copy-start(s32[1,1,32,2]{2,3,1,0:T(2,128)} %param.12) | copy-start | bytes 772
  0.6 52.5 %collective-permute-start.6 = (bf16[8,4,256,256]{3,2,1,0:T(8,128)(2,1)}, bf16[8,4,256,256]{3,2,1,0:T(8,128)(2,1)}, u32[]{:S(2)}, u32[]{:S(2)}) collective-permute-start(bf16[8,4,256,256]{3,2,1,0:T(8,128)(2,1)} %a_ref.3), channel_id=1, source_target_pairs={{0,1},{1,0},{2,3},{3,2},{4,5},{5,4},{6,7},{7,6},{8,9},{9,8},{10,11... | collective-permute-start | bytes 12582920 | tf_op jit(solution)/shard_map/ppermute | solution.py:271
  0.7 14.4 %collective-permute-start = (s32[4,8]{1,0:T(4,128)}, s32[4,8]{1,0:T(4,128)S(1)}, u32[]{:S(2)}, u32[]{:S(2)}) collective-permute-start(s32[4,8]{1,0:T(4,128)} %bitcast.21), channel_id=1, source_target_pairs={{0,1},{1,0},{2,3},{3,2},{4,5},{5,4},{6,7},{7,6},{8,9},{9,8},{10,11... | collective-permute-start | bytes 392 | tf_op jit(solution)/shard_map/ppermute | solution.py:259
  2.6 19.7 %all-to-all-start = ((s32[32,1,2]{2,1,0:T(1,128)}), s32[32,1,2]{2,1,0:T(1,128)S(1)}, u32[]{:S(2)}, u32[]{:S(2)}) async-start(s32[32,1,2]{2,1,0:T(1,128)} %copy.10), calls=%async_computation | async-start | bytes 32768 | tf_op jit(solution)/shard_map/all_to_all | solution.py:254
  15.1 38.0 %copy-start.2 = (bf16[32,2048]{1,0:T(8,128)(2,1)S(1)}, bf16[32,2048]{1,0:T(8,128)(2,1)}, u32[]{:S(2)}) copy-start(bf16[32,2048]{1,0:T(8,128)(2,1)} %current) | copy-start | bytes 393220
  15.1 38.0 %copy-start.5 = (s32[8,4]{0,1:T(4,128)S(1)}, s32[8,4]{0,1:T(4,128)}, u32[]{:S(2)}) copy-start(s32[8,4]{0,1:T(4,128)} %param.10) | copy-start | bytes 388
  24.0 21.4 %all-to-all-start.1 = ((bf16[32,64,128]{2,1,0:T(8,128)(2,1)}), bf16[32,64,128]{2,1,0:T(8,128)(2,1)S(1)}, u32[]{:S(2)}, u32[]{:S(2)}) async-start(bf16[32,64,128]{2,1,0:T(8,128)(2,1)} %bitcast.5), calls=%async_computation.1 | async-start | bytes 1048576 | tf_op jit(solution)/shard_map/all_to_all | solution.py:280
  28.9 22.8 %collective-permute-start.5 = (bf16[32,2048]{1,0:T(8,128)(2,1)}, bf16[32,2048]{1,0:T(8,128)(2,1)S(1)}, u32[]{:S(2)}, u32[]{:S(2)}) collective-permute-start(bf16[32,2048]{1,0:T(8,128)(2,1)} %current), channel_id=1, source_target_pairs={{2,0},{4,2},{6,4},{8,6},{10,8},{12,10},{14,12},{16,14},{18,16},{20... | collective-permute-start | bytes 393224 | tf_op jit(solution)/shard_map/ppermute | solution.py:278
  35.9 17.2 %collective-permute-start.4 = (bf16[32,2048]{1,0:T(8,128)(2,1)}, bf16[32,2048]{1,0:T(8,128)(2,1)S(1)}, u32[]{:S(2)}, u32[]{:S(2)}) collective-permute-start(bf16[32,2048]{1,0:T(8,128)(2,1)} %current), channel_id=1, source_target_pairs={{0,2},{2,4},{4,6},{6,8},{8,10},{10,12},{12,14},{14,16},{16,18},{18... | collective-permute-start | bytes 393224 | tf_op jit(solution)/shard_map/ppermute | solution.py:277
  47.3 11.7 %collective-permute-start.1 = (bf16[8,32,128]{2,1,0:T(8,128)(2,1)}, bf16[8,32,128]{2,1,0:T(8,128)(2,1)S(1)}, u32[]{:S(2)}, u32[]{:S(2)}) collective-permute-start(bf16[8,32,128]{2,1,0:T(8,128)(2,1)} %get-tuple-element.21), channel_id=1, source_target_pairs={{0,2},{2,4},{4,6},{6,0},{1,3},{3,5},{5,7},{7,1},{8,10},{10,12},{12... | collective-permute-start | bytes 196616 | tf_op jit(solution)/shard_map/ppermute | solution.py:289
  48.8 10.2 %collective-permute-start.2 = (bf16[8,32,128]{2,1,0:T(8,128)(2,1)S(1)}, bf16[8,32,128]{2,1,0:T(8,128)(2,1)S(1)}, u32[]{:S(2)}, u32[]{:S(2)}) collective-permute-start(bf16[8,32,128]{2,1,0:T(8,128)(2,1)S(1)} %get-tuple-element.22), channel_id=1, source_target_pairs={{0,4},{2,6},{4,0},{6,2},{1,5},{3,7},{5,1},{7,3},{8,12},{10,14},{12... | collective-permute-start | bytes 196616 | tf_op jit(solution)/shard_map/ppermute | solution.py:289
  51.7 7.3 %collective-permute-start.3 = (bf16[8,32,128]{2,1,0:T(8,128)(2,1)S(1)}, bf16[8,32,128]{2,1,0:T(8,128)(2,1)S(1)}, u32[]{:S(2)}, u32[]{:S(2)}) collective-permute-start(bf16[8,32,128]{2,1,0:T(8,128)(2,1)S(1)} %get-tuple-element.23), channel_id=1, source_target_pairs={{0,6},{2,0},{4,2},{6,4},{1,7},{3,1},{5,3},{7,5},{8,14},{10,8},{12,... | collective-permute-start | bytes 196616 | tf_op jit(solution)/shard_map/ppermute | solution.py:289
  53.1 5.9 %copy-start = (bf16[8,256,128]{2,1,0:T(8,128)(2,1)S(1)}, bf16[8,256,128]{2,1,0:T(8,128)(2,1)}, u32[]{:S(2)}) copy-start(bf16[8,256,128]{2,1,0:T(8,128)(2,1)} %refs_5_.1) | copy-start | bytes 1572868
  53.1 5.9 %copy-start.1 = (bf16[8,256,128]{2,1,0:T(8,128)(2,1)S(1)}, bf16[8,256,128]{2,1,0:T(8,128)(2,1)}, u32[]{:S(2)}) copy-start(bf16[8,256,128]{2,1,0:T(8,128)(2,1)} %refs_3_.3) | copy-start | bytes 1572868
  61.7 0.8 copy-start.3
  62.5 20.5 %all-to-all-start.2 = ((bf16[32,64,128]{2,1,0:T(8,128)(2,1)}), bf16[32,64,128]{2,1,0:T(8,128)(2,1)S(1)}, u32[]{:S(2)}, u32[]{:S(2)}) async-start(bf16[32,64,128]{2,1,0:T(8,128)(2,1)} %bitcast.20), calls=%async_computation.2 | async-start | bytes 1048576 | tf_op jit(solution)/shard_map/all_to_all | solution.py:280
  67.8 20.7 %collective-permute-start.11 = (bf16[32,2048]{1,0:T(8,128)(2,1)}, bf16[32,2048]{1,0:T(8,128)(2,1)S(1)}, u32[]{:S(2)}, u32[]{:S(2)}) collective-permute-start(bf16[32,2048]{1,0:T(8,128)(2,1)} %get-tuple-element.33.current), channel_id=1, source_target_pairs={{2,0},{4,2},{6,4},{8,6},{10,8},{12,10},{14,12},{16,14},{18,16},{20... | collective-permute-start | bytes 393224 | tf_op jit(solution)/shard_map/ppermute | solution.py:278
  72.4 16.2 %collective-permute-start.10 = (bf16[32,2048]{1,0:T(8,128)(2,1)}, bf16[32,2048]{1,0:T(8,128)(2,1)S(1)}, u32[]{:S(2)}, u32[]{:S(2)}) collective-permute-start(bf16[32,2048]{1,0:T(8,128)(2,1)} %get-tuple-element.33.current), channel_id=1, source_target_pairs={{0,2},{2,4},{4,6},{6,8},{8,10},{10,12},{12,14},{14,16},{16,18},{18... | collective-permute-start | bytes 393224 | tf_op jit(solution)/shard_map/ppermute | solution.py:277
  84.3 11.0 %collective-permute-start.7 = (bf16[8,32,128]{2,1,0:T(8,128)(2,1)S(1)}, bf16[8,32,128]{2,1,0:T(8,128)(2,1)S(1)}, u32[]{:S(2)}, u32[]{:S(2)}) collective-permute-start(bf16[8,32,128]{2,1,0:T(8,128)(2,1)S(1)} %get-tuple-element.30), channel_id=1, source_target_pairs={{0,2},{2,4},{4,6},{6,0},{1,3},{3,5},{5,7},{7,1},{8,10},{10,12},{12... | collective-permute-start | bytes 196616 | tf_op jit(solution)/shard_map/ppermute | solution.py:289
  85.6 9.7 %collective-permute-start.8 = (bf16[8,32,128]{2,1,0:T(8,128)(2,1)S(1)}, bf16[8,32,128]{2,1,0:T(8,128)(2,1)S(1)}, u32[]{:S(2)}, u32[]{:S(2)}) collective-permute-start(bf16[8,32,128]{2,1,0:T(8,128)(2,1)S(1)} %get-tuple-element.31), channel_id=1, source_target_pairs={{0,4},{2,6},{4,0},{6,2},{1,5},{3,7},{5,1},{7,3},{8,12},{10,14},{12... | collective-permute-start | bytes 196616 | tf_op jit(solution)/shard_map/ppermute | solution.py:289
  86.3 9.1 %collective-permute-start.9 = (bf16[8,32,128]{2,1,0:T(8,128)(2,1)S(1)}, bf16[8,32,128]{2,1,0:T(8,128)(2,1)S(1)}, u32[]{:S(2)}, u32[]{:S(2)}) collective-permute-start(bf16[8,32,128]{2,1,0:T(8,128)(2,1)S(1)} %get-tuple-element.32), channel_id=1, source_target_pairs={{0,6},{2,0},{4,2},{6,4},{1,7},{3,1},{5,3},{7,5},{8,14},{10,8},{12,... | collective-permute-start | bytes 196616 | tf_op jit(solution)/shard_map/ppermute | solution.py:289
  88.6 0.9 copy-start.4

commit v3 on v2

--- a/solution.py
+++ b/solution.py
@@ -1,5 +1,3 @@
-import functools
-
 import jax
 import jax.numpy as jnp
 from jax import lax
@@ -126,11 +124,15 @@
 
 
 def near_kernel(
-    first_ref, here, there, before, current, after, a_ref, b_ref, out_ref,
+    first_ref, here, there, before, after, current_ref, a_ref, b_ref, out_ref,
     window, a_held, b_held, turned, sems,
 ):
     clusters, slots, leaf = a_ref.shape[0], a_ref.shape[1], a_ref.shape[2]
-    width = current.shape[1]
+    width = before.shape[1]
+    middle = pltpu.make_async_copy(
+        current_ref, window.at[:, pl.ds(width, width)], sems.at[2 * clusters]
+    )
+    middle.start()
     copies = []
     for c in range(clusters):
         for source, held in ((a_ref, a_held), (b_ref, b_held)):
@@ -139,11 +141,13 @@
             )
     for copy in copies:
         copy.start()
-    for k, piece in enumerate((before, current, after)):
-        window[:, k * width : (k + 1) * width] = piece[...]
+    window[:, :width] = before[...]
+    window[:, 2 * width :] = after[...]
     first = first_ref[0]
+    middle.wait()
     for c in range(clusters):
-        total = 0.5 * current[:, c * leaf : (c + 1) * leaf].astype(jnp.float32)
+        at = width + c * leaf
+        total = 0.5 * window[:, at : at + leaf].astype(jnp.float32)
         for k, (cols, held) in enumerate(((here, a_held), (there, b_held))):
             copies[2 * c + k].wait()
             for s in range(slots):
@@ -160,19 +164,19 @@
     return pl.pallas_call(
         near_kernel,
         out_shape=jax.ShapeDtypeStruct((clusters, cols, leaf), jnp.float32),
-        in_specs=[SMEM] * 3 + [VMEM] * 3 + [HBM] * 2,
+        in_specs=[SMEM] * 3 + [VMEM] * 2 + [HBM] * 3,
         out_specs=VMEM,
         scratch_shapes=[
             pltpu.VMEM((cols, 3 * width), current.dtype),
             pltpu.VMEM(a.shape, a.dtype),
             pltpu.VMEM(b.shape, b.dtype),
             pltpu.VMEM((2, 2 * slots, leaf, leaf), a.dtype),
-            pltpu.SemaphoreType.DMA((2 * clusters,)),
+            pltpu.SemaphoreType.DMA((2 * clusters + 1,)),
         ],
         compiler_params=params(16),
         cost_estimate=cost(4 * clusters * slots * cols * leaf * leaf, 9_000_000),
         name="near",
-    )(first, here, there, before, current, after, in_hbm(a), in_hbm(b))
+    )(first, here, there, before, after, in_hbm(current), in_hbm(a), in_hbm(b))
 
 
 def image_into(c, own, parts, row_basis, near, image):
@@ -224,7 +228,7 @@
         middle_kernel,
         out_shape=[
             jax.ShapeDtypeStruct((cols, clusters * row_basis.shape[1]), dtype),
-            jax.ShapeDtypeStruct((pairs, cols, rank), dtype),
+            pltpu.HBM((pairs, cols, rank), dtype),
         ],
         in_specs=[SMEM] + [VMEM] * (len(parts) + 4),
         out_specs=[VMEM, VMEM],
@@ -284,7 +288,8 @@
             first, our_cols, their_cols, before, current, after, near_blocks, theirs
         )
         moved = []
-        for step, part in enumerate(parts, 1):
+        for step in (1, 3, 2):
+            part = parts[step - 1]
             ring = [(i, (i + step) % col_peers) for i in range(col_peers)]
             moved.append(lax.ppermute(part, "col", ring))
         return own, moved, near

time: 96.8 us -> 94.8 us (0.979)
  local copies, waits for them, and re-layouts: 3.1 us -> 1.39 us
    unnamed x14 -> x8, local copies, waits for them, and re-layouts: 1.73 us -> 0.02 us
where the time goes in v3:
time: 94.8 us; the launch traced here: 94 us
  starting transfers between devices  47.6 us (50%)
  Pallas kernels  23.4 us (25%)
  waiting for transfers between devices  19.5 us (21%)
  local copies, waits for them, and re-layouts  1.39 us (1%)
  matrix products  1.32 us (1%)
    all_to_all x2, waiting for transfers between devices, exchanges(): picked = lax.all_to_all(blocks, 'row', 0, 0, tiled=True)  12.3 us
    pallas_call x2, Pallas kernels, near_terms(): pl.pallas_call(near_kernel, out_shape=jax.ShapeDtypeStruct((clusters, col...  11.9 us
    ppermute x2, starting transfers between devices, exchanges(): after = lax.ppermute(current, ('row', 'col'), down)  11.6 us
    all_to_all x1, starting transfers between devices, per_device(): lax.all_to_all(far_src.reshape(row_peers, 1, slot_count), 'row', 0, 0, ti...  11.2 us
    all_to_all x2, starting transfers between devices, exchanges(): picked = lax.all_to_all(blocks, 'row', 0, 0, tiled=True)  10.8 us
    ppermute x6, starting transfers between devices, exchanges(): moved.append(lax.ppermute(part, 'col', ring))  9.48 us
    all_to_all x1, waiting for transfers between devices, per_device(): lax.all_to_all(far_src.reshape(row_peers, 1, slot_count), 'row', 0, 0, ti...  7.17 us
    ppermute x2, starting transfers between devices, exchanges(): before = lax.ppermute(current, ('row', 'col'), up)  3.84 us
  transfers between devices with their start and end apart: 15, of which 3 were waited for; matrix products, arithmetic and copies ran while one was open for 3% of the time, Pallas kernels for 21%

profile of v3, /device:TPU:32, one launch (start us, length us, event | category | flops | bytes accessed | tf_op | source)
XLA Modules:
  0.0 94.0 jit_solution(16457380932288199963)
XLA Ops:
  0.6 0.1 collective-permute-start.6
  0.7 0.5 collective-permute-start
  1.2 1.4 %copy.10 = s32[32,1,2]{2,1,0:T(1,128)} copy(s32[32,1,2]{0,2,1:T(2,128)} %bitcast.27) | data formatting | bytes 512 | tf_op jit(solution)/shard_map/reshape | solution.py:258
  2.6 11.2 %all-to-all-start = ((s32[32,1,2]{2,1,0:T(1,128)}), s32[32,1,2]{2,1,0:T(1,128)S(1)}, u32[]{:S(2)}, u32[]{:S(2)}) async-start(s32[32,1,2]{2,1,0:T(1,128)} %copy.10), calls=%async_computation | async-start | bytes 32768 | tf_op jit(solution)/shard_map/all_to_all | solution.py:258
  13.8 1.3 %convolution_convert_fusion.coeffs_ref = bf16[8,32,128]{2,1,0:T(8,128)(2,1)S(1)} fusion(bf16[8,256,128]{2,1,0:T(8,128)(2,1)} %refs_5_.1, bf16[4,8,8,256]{3,2,1,0:T(8,128)(2,1)} %bitcast.25), kind=kOutput, calls=%fused_computation | convolution fusion | flops 16809984 | bytes 720896 | tf_op jit(solution)/shard_map/sao,aon->asn/dot_general | solution.py:271
  15.1 0.0 copy-start.2
  15.1 0.0 collective-permute-done.there
  15.2 7.2 %all-to-all-done.wanted_ref = s32[32,1,2]{2,1,0:T(1,128)S(1)} async-done(((s32[32,1,2]{2,1,0:T(1,128)}), s32[32,1,2]{2,1,0:T(1,128)S(1)}, u32[]{:S(2)}, u32[]{:S(2)}) %all-to-all-start) | async-done | bytes 288 | tf_op jit(solution)/shard_map/all_to_all | solution.py:258
  22.3 1.7 %pick.1 = bf16[64,32,128]{2,1,0:T(8,128)(2,1)} custom-call(s32[32,1,2]{2,1,0:T(1,128)S(1)} %all-to-all-done.wanted_ref, bf16[8,32,128]{2,1,0:T(8,128)(2,1)S(1)} %convolution_convert_fusion.coeffs_ref), custom_call_target="tpu_custom_call" | custom-call | bytes 600000 | tf_op jit(solution)/shard_map/pick/pallas_call | solution.py:83
  24.0 4.9 %all-to-all-start.1 = ((bf16[32,64,128]{2,1,0:T(8,128)(2,1)}), bf16[32,64,128]{2,1,0:T(8,128)(2,1)S(1)}, u32[]{:S(2)}, u32[]{:S(2)}) async-start(bf16[32,64,128]{2,1,0:T(8,128)(2,1)} %bitcast.5), calls=%async_computation.1 | async-start | bytes 1048576 | tf_op jit(solution)/shard_map/all_to_all | solution.py:284
  28.9 7.0 %collective-permute-start.5 = (bf16[32,2048]{1,0:T(8,128)(2,1)}, bf16[32,2048]{1,0:T(8,128)(2,1)S(1)}, u32[]{:S(2)}, u32[]{:S(2)}) collective-permute-start(bf16[32,2048]{1,0:T(8,128)(2,1)} %current_ref), channel_id=1, source_target_pairs={{2,0},{4,2},{6,4},{8,6},{10,8},{12,10},{14,12},{16,14},{18,16},{20... | collective-permute-start | bytes 393224 | tf_op jit(solution)/shard_map/ppermute | solution.py:282
  36.0 1.9 %collective-permute-start.4 = (bf16[32,2048]{1,0:T(8,128)(2,1)}, bf16[32,2048]{1,0:T(8,128)(2,1)S(1)}, u32[]{:S(2)}, u32[]{:S(2)}) collective-permute-start(bf16[32,2048]{1,0:T(8,128)(2,1)} %current_ref), channel_id=1, source_target_pairs={{0,2},{2,4},{4,6},{6,8},{8,10},{10,12},{12,14},{14,16},{16,18},{18... | collective-permute-start | bytes 393224 | tf_op jit(solution)/shard_map/ppermute | solution.py:281
  37.9 3.4 %stage.1.couple_ref = bf16[32,2,128,128]{3,2,1,0:T(8,128)(2,1)S(1)} custom-call(bf16[32,2,128,128]{3,2,1,0:T(8,128)(2,1)} %bitcast.24), custom_call_target="tpu_custom_call" | custom-call | bytes 4194304 | tf_op jit(solution)/shard_map/stage/pallas_call | solution.py:57
  41.3 4.1 %all-to-all-done.1 = bf16[32,64,128]{2,1,0:T(8,128)(2,1)S(1)} async-done(((bf16[32,64,128]{2,1,0:T(8,128)(2,1)}), bf16[32,64,128]{2,1,0:T(8,128)(2,1)S(1)}, u32[]{:S(2)}, u32[]{:S(2)}) %all-to-all-start.1) | async-done | bytes 524320 | tf_op jit(solution)/shard_map/all_to_all | solution.py:284
  45.4 1.2 %couple.2 = (f32[8,32,128]{2,1,0:T(8,128)S(1)}, bf16[8,32,128]{2,1,0:T(8,128)(2,1)S(1)}, bf16[8,32,128]{2,1,0:T(8,128)(2,1)S(1)}, bf16[8,32,128]{2,1,0:T(8,128)(2,1)S(1)}) custom-call(s32[1]{0:T(128)} %bitcast.2.place_ref, s32[2,32]{1,0:T(2,128)S(1)} %bitcast.22, bf16[64,32,128]{2,1,0:T(8,128)(2,1)S(1)} %bitcast.17, ...), custom_call_target="tpu_custom_call" | custom-call | flops 67108864 | bytes 4000000 | tf_op jit(solution)/shard_map/couple/pallas_call | solution.py:114
  46.7 1.7 %collective-permute-start.1 = (bf16[8,32,128]{2,1,0:T(8,128)(2,1)S(1)}, bf16[8,32,128]{2,1,0:T(8,128)(2,1)S(1)}, u32[]{:S(2)}, u32[]{:S(2)}) collective-permute-start(bf16[8,32,128]{2,1,0:T(8,128)(2,1)S(1)} %get-tuple-element.21), channel_id=1, source_target_pairs={{0,2},{2,4},{4,6},{6,0},{1,3},{3,5},{5,7},{7,1},{8,10},{10,12},{12... | collective-permute-start | bytes 196616 | tf_op jit(solution)/shard_map/ppermute | solution.py:294
  48.3 1.7 %collective-permute-start.2 = (bf16[8,32,128]{2,1,0:T(8,128)(2,1)S(1)}, bf16[8,32,128]{2,1,0:T(8,128)(2,1)S(1)}, u32[]{:S(2)}, u32[]{:S(2)}) collective-permute-start(bf16[8,32,128]{2,1,0:T(8,128)(2,1)S(1)} %get-tuple-element.22), channel_id=1, source_target_pairs={{0,6},{2,0},{4,2},{6,4},{1,7},{3,1},{5,3},{7,5},{8,14},{10,8},{12,... | collective-permute-start | bytes 196616 | tf_op jit(solution)/shard_map/ppermute | solution.py:294
  50.0 2.0 %collective-permute-start.3 = (bf16[8,32,128]{2,1,0:T(8,128)(2,1)S(1)}, bf16[8,32,128]{2,1,0:T(8,128)(2,1)S(1)}, u32[]{:S(2)}, u32[]{:S(2)}) collective-permute-start(bf16[8,32,128]{2,1,0:T(8,128)(2,1)S(1)} %get-tuple-element.23), channel_id=1, source_target_pairs={{0,4},{2,6},{4,0},{6,2},{1,5},{3,7},{5,1},{7,3},{8,12},{10,14},{12... | collective-permute-start | bytes 196616 | tf_op jit(solution)/shard_map/ppermute | solution.py:294
  52.0 0.0 copy-start
  52.0 0.0 copy-start.1
  52.0 5.9 %near.2.refs_4_ = f32[8,32,256]{2,1,0:T(8,128)S(1)} custom-call(s32[1]{0:T(128)} %bitcast.8.first_ref, s32[4,8]{1,0:T(4,128)S(1)} %bitcast.20, s32[4,8]{1,0:T(4,128)S(1)} %collective-permute-done.there, bf16[32,2048]{1,0:T(8,128)(2,1)S(1)} %collective-permute-done.4.before, bf16[32,2048]{1,0:T(8,128)(2,1)S(1)} %collective-permute-done.5.after, ...), custom_call_target="tpu_custom_call" | custom-call | flops 268435456 | bytes 9000000 | tf_op jit(solution)/shard_map/near/pallas_call | solution.py:164
  58.0 3.0 %finish_and_pick.1 = (bf16[32,2048]{1,0:T(8,128)(2,1)}, bf16[64,32,128]{2,1,0:T(8,128)(2,1)}) custom-call(s32[32,1,2]{2,1,0:T(1,128)S(1)} %all-to-all-done.wanted_ref, f32[8,32,128]{2,1,0:T(8,128)S(1)} %get-tuple-element.20.own, bf16[8,32,128]{2,1,0:T(8,128)(2,1)S(1)} %collective-permute-done.1.refs_0_, ...), custom_call_target="tpu_custom_call" | custom-call | flops 40000000 | bytes 2500000 | tf_op jit(solution)/shard_map/finish_and_pick/pallas_call | solution.py:227
  61.0 5.9 %all-to-all-start.2 = ((bf16[32,64,128]{2,1,0:T(8,128)(2,1)}), bf16[32,64,128]{2,1,0:T(8,128)(2,1)S(1)}, u32[]{:S(2)}, u32[]{:S(2)}) async-start(bf16[32,64,128]{2,1,0:T(8,128)(2,1)} %bitcast.26), calls=%async_computation.2 | async-start | bytes 1048576 | tf_op jit(solution)/shard_map/all_to_all | solution.py:284
  66.9 4.6 %collective-permute-start.11 = (bf16[32,2048]{1,0:T(8,128)(2,1)}, bf16[32,2048]{1,0:T(8,128)(2,1)S(1)}, u32[]{:S(2)}, u32[]{:S(2)}) collective-permute-start(bf16[32,2048]{1,0:T(8,128)(2,1)} %get-tuple-element.33.current_ref), channel_id=1, source_target_pairs={{2,0},{4,2},{6,4},{8,6},{10,8},{12,10},{14,12},{16,14},{18,16},{20... | collective-permute-start | bytes 393224 | tf_op jit(solution)/shard_map/ppermute | solution.py:282
  71.5 1.9 %collective-permute-start.10 = (bf16[32,2048]{1,0:T(8,128)(2,1)}, bf16[32,2048]{1,0:T(8,128)(2,1)S(1)}, u32[]{:S(2)}, u32[]{:S(2)}) collective-permute-start(bf16[32,2048]{1,0:T(8,128)(2,1)} %get-tuple-element.33.current_ref), channel_id=1, source_target_pairs={{0,2},{2,4},{4,6},{6,8},{8,10},{10,12},{12,14},{14,16},{16,18},{18... | collective-permute-start | bytes 393224 | tf_op jit(solution)/shard_map/ppermute | solution.py:281
  73.4 8.3 %all-to-all-done.2 = bf16[32,64,128]{2,1,0:T(8,128)(2,1)S(1)} async-done(((bf16[32,64,128]{2,1,0:T(8,128)(2,1)}), bf16[32,64,128]{2,1,0:T(8,128)(2,1)S(1)}, u32[]{:S(2)}, u32[]{:S(2)}) %all-to-all-start.2) | async-done | bytes 524320 | tf_op jit(solution)/shard_map/all_to_all | solution.py:284
  81.7 1.2 %couple.3 = (f32[8,32,128]{2,1,0:T(8,128)S(1)}, bf16[8,32,128]{2,1,0:T(8,128)(2,1)S(1)}, bf16[8,32,128]{2,1,0:T(8,128)(2,1)S(1)}, bf16[8,32,128]{2,1,0:T(8,128)(2,1)S(1)}) custom-call(s32[1]{0:T(128)} %bitcast.2.place_ref, s32[2,32]{1,0:T(2,128)S(1)} %bitcast.23, bf16[64,32,128]{2,1,0:T(8,128)(2,1)S(1)} %bitcast.18, ...), custom_call_target="tpu_custom_call" | custom-call | flops 67108864 | bytes 4000000 | tf_op jit(solution)/shard_map/couple/pallas_call | solution.py:114
  82.9 1.1 %collective-permute-start.7 = (bf16[8,32,128]{2,1,0:T(8,128)(2,1)S(1)}, bf16[8,32,128]{2,1,0:T(8,128)(2,1)S(1)}, u32[]{:S(2)}, u32[]{:S(2)}) collective-permute-start(bf16[8,32,128]{2,1,0:T(8,128)(2,1)S(1)} %get-tuple-element.30), channel_id=1, source_target_pairs={{0,2},{2,4},{4,6},{6,0},{1,3},{3,5},{5,7},{7,1},{8,10},{10,12},{12... | collective-permute-start | bytes 196616 | tf_op jit(solution)/shard_map/ppermute | solution.py:294
  84.1 2.2 %collective-permute-start.8 = (bf16[8,32,128]{2,1,0:T(8,128)(2,1)S(1)}, bf16[8,32,128]{2,1,0:T(8,128)(2,1)S(1)}, u32[]{:S(2)}, u32[]{:S(2)}) collective-permute-start(bf16[8,32,128]{2,1,0:T(8,128)(2,1)S(1)} %get-tuple-element.31), channel_id=1, source_target_pairs={{0,6},{2,0},{4,2},{6,4},{1,7},{3,1},{5,3},{7,5},{8,14},{10,8},{12,... | collective-permute-start | bytes 196616 | tf_op jit(solution)/shard_map/ppermute | solution.py:294
  86.2 0.9 collective-permute-start.9
  87.1 5.9 %near.3.refs_4_ = f32[8,32,256]{2,1,0:T(8,128)S(1)} custom-call(s32[1]{0:T(128)} %bitcast.8.first_ref, s32[4,8]{1,0:T(4,128)S(1)} %bitcast.21, s32[4,8]{1,0:T(4,128)S(1)} %collective-permute-done.there, bf16[32,2048]{1,0:T(8,128)(2,1)S(1)} %collective-permute-done.10.before, bf16[32,2048]{1,0:T(8,128)(2,1)S(1)} %collective-permute-done.11.after, ...), custom_call_target="tpu_custom_call" | custom-call | flops 268435456 | bytes 9000000 | tf_op jit(solution)/shard_map/near/pallas_call | solution.py:164
  93.1 0.9 %finish.1 = bf16[32,2048]{1,0:T(8,128)(2,1)} custom-call(f32[8,32,128]{2,1,0:T(8,128)S(1)} %get-tuple-element.29.own, bf16[8,32,128]{2,1,0:T(8,128)(2,1)S(1)} %collective-permute-done.7.refs_0_, bf16[8,32,128]{2,1,0:T(8,128)(2,1)S(1)} %collective-permute-done.8.refs_1_, bf16[8,32,128]{2,1,0:T(8,128)(2,1)S(1)} %collective-permute-done.9.refs_2_, ...), custom_call_target="tpu_custom_call" | custom-call | flops 20000000 | bytes 1500000 | tf_op jit(solution)/shard_map/finish/pallas_call | solution.py:212
  (16 shorter events, 0.0 us)
Async XLA Ops:
  0.6 44.8 %copy-start.3 = (s32[1,1,32,2]{2,3,1,0:T(2,128)S(1)}, s32[1,1,32,2]{2,3,1,0:T(2,128)}, u32[]{:S(2)}) copy-start(s32[1,1,32,2]{2,3,1,0:T(2,128)} %param.12) | copy-start | bytes 772
  0.6 51.3 %collective-permute-start.6 = (bf16[8,4,256,256]{3,2,1,0:T(8,128)(2,1)}, bf16[8,4,256,256]{3,2,1,0:T(8,128)(2,1)}, u32[]{:S(2)}, u32[]{:S(2)}) collective-permute-start(bf16[8,4,256,256]{3,2,1,0:T(8,128)(2,1)} %a_ref.3), channel_id=1, source_target_pairs={{0,1},{1,0},{2,3},{3,2},{4,5},{5,4},{6,7},{7,6},{8,9},{9,8},{10,11... | collective-permute-start | bytes 12582920 | tf_op jit(solution)/shard_map/ppermute | solution.py:275
  0.7 14.4 %collective-permute-start = (s32[4,8]{1,0:T(4,128)}, s32[4,8]{1,0:T(4,128)S(1)}, u32[]{:S(2)}, u32[]{:S(2)}) collective-permute-start(s32[4,8]{1,0:T(4,128)} %bitcast.19), channel_id=1, source_target_pairs={{0,1},{1,0},{2,3},{3,2},{4,5},{5,4},{6,7},{7,6},{8,9},{9,8},{10,11... | collective-permute-start | bytes 392 | tf_op jit(solution)/shard_map/ppermute | solution.py:263
  2.6 19.7 %all-to-all-start = ((s32[32,1,2]{2,1,0:T(1,128)}), s32[32,1,2]{2,1,0:T(1,128)S(1)}, u32[]{:S(2)}, u32[]{:S(2)}) async-start(s32[32,1,2]{2,1,0:T(1,128)} %copy.10), calls=%async_computation | async-start | bytes 32768 | tf_op jit(solution)/shard_map/all_to_all | solution.py:258
  15.1 36.8 %copy-start.2 = (s32[8,4]{0,1:T(4,128)S(1)}, s32[8,4]{0,1:T(4,128)}, u32[]{:S(2)}) copy-start(s32[8,4]{0,1:T(4,128)} %param.10) | copy-start | bytes 388
  24.0 21.4 %all-to-all-start.1 = ((bf16[32,64,128]{2,1,0:T(8,128)(2,1)}), bf16[32,64,128]{2,1,0:T(8,128)(2,1)S(1)}, u32[]{:S(2)}, u32[]{:S(2)}) async-start(bf16[32,64,128]{2,1,0:T(8,128)(2,1)} %bitcast.5), calls=%async_computation.1 | async-start | bytes 1048576 | tf_op jit(solution)/shard_map/all_to_all | solution.py:284
  28.9 21.1 %collective-permute-start.5 = (bf16[32,2048]{1,0:T(8,128)(2,1)}, bf16[32,2048]{1,0:T(8,128)(2,1)S(1)}, u32[]{:S(2)}, u32[]{:S(2)}) collective-permute-start(bf16[32,2048]{1,0:T(8,128)(2,1)} %current_ref), channel_id=1, source_target_pairs={{2,0},{4,2},{6,4},{8,6},{10,8},{12,10},{14,12},{16,14},{18,16},{20... | collective-permute-start | bytes 393224 | tf_op jit(solution)/shard_map/ppermute | solution.py:282
  36.0 16.0 %collective-permute-start.4 = (bf16[32,2048]{1,0:T(8,128)(2,1)}, bf16[32,2048]{1,0:T(8,128)(2,1)S(1)}, u32[]{:S(2)}, u32[]{:S(2)}) collective-permute-start(bf16[32,2048]{1,0:T(8,128)(2,1)} %current_ref), channel_id=1, source_target_pairs={{0,2},{2,4},{4,6},{6,8},{8,10},{10,12},{12,14},{14,16},{16,18},{18... | collective-permute-start | bytes 393224 | tf_op jit(solution)/shard_map/ppermute | solution.py:281
  46.7 11.3 %collective-permute-start.1 = (bf16[8,32,128]{2,1,0:T(8,128)(2,1)S(1)}, bf16[8,32,128]{2,1,0:T(8,128)(2,1)S(1)}, u32[]{:S(2)}, u32[]{:S(2)}) collective-permute-start(bf16[8,32,128]{2,1,0:T(8,128)(2,1)S(1)} %get-tuple-element.21), channel_id=1, source_target_pairs={{0,2},{2,4},{4,6},{6,0},{1,3},{3,5},{5,7},{7,1},{8,10},{10,12},{12... | collective-permute-start | bytes 196616 | tf_op jit(solution)/shard_map/ppermute | solution.py:294
  48.3 9.6 %collective-permute-start.2 = (bf16[8,32,128]{2,1,0:T(8,128)(2,1)S(1)}, bf16[8,32,128]{2,1,0:T(8,128)(2,1)S(1)}, u32[]{:S(2)}, u32[]{:S(2)}) collective-permute-start(bf16[8,32,128]{2,1,0:T(8,128)(2,1)S(1)} %get-tuple-element.22), channel_id=1, source_target_pairs={{0,6},{2,0},{4,2},{6,4},{1,7},{3,1},{5,3},{7,5},{8,14},{10,8},{12,... | collective-permute-start | bytes 196616 | tf_op jit(solution)/shard_map/ppermute | solution.py:294
  50.0 8.0 %collective-permute-start.3 = (bf16[8,32,128]{2,1,0:T(8,128)(2,1)S(1)}, bf16[8,32,128]{2,1,0:T(8,128)(2,1)S(1)}, u32[]{:S(2)}, u32[]{:S(2)}) collective-permute-start(bf16[8,32,128]{2,1,0:T(8,128)(2,1)S(1)} %get-tuple-element.23), channel_id=1, source_target_pairs={{0,4},{2,6},{4,0},{6,2},{1,5},{3,7},{5,1},{7,3},{8,12},{10,14},{12... | collective-permute-start | bytes 196616 | tf_op jit(solution)/shard_map/ppermute | solution.py:294
  52.0 6.0 %copy-start = (bf16[8,256,128]{2,1,0:T(8,128)(2,1)S(1)}, bf16[8,256,128]{2,1,0:T(8,128)(2,1)}, u32[]{:S(2)}) copy-start(bf16[8,256,128]{2,1,0:T(8,128)(2,1)} %refs_5_.1) | copy-start | bytes 1572868
  52.0 6.0 %copy-start.1 = (bf16[8,256,128]{2,1,0:T(8,128)(2,1)S(1)}, bf16[8,256,128]{2,1,0:T(8,128)(2,1)}, u32[]{:S(2)}) copy-start(bf16[8,256,128]{2,1,0:T(8,128)(2,1)} %refs_3_.3) | copy-start | bytes 1572868
  61.0 20.7 %all-to-all-start.2 = ((bf16[32,64,128]{2,1,0:T(8,128)(2,1)}), bf16[32,64,128]{2,1,0:T(8,128)(2,1)S(1)}, u32[]{:S(2)}, u32[]{:S(2)}) async-start(bf16[32,64,128]{2,1,0:T(8,128)(2,1)} %bitcast.26), calls=%async_computation.2 | async-start | bytes 1048576 | tf_op jit(solution)/shard_map/all_to_all | solution.py:284
  66.9 20.2 %collective-permute-start.11 = (bf16[32,2048]{1,0:T(8,128)(2,1)}, bf16[32,2048]{1,0:T(8,128)(2,1)S(1)}, u32[]{:S(2)}, u32[]{:S(2)}) collective-permute-start(bf16[32,2048]{1,0:T(8,128)(2,1)} %get-tuple-element.33.current_ref), channel_id=1, source_target_pairs={{2,0},{4,2},{6,4},{8,6},{10,8},{12,10},{14,12},{16,14},{18,16},{20... | collective-permute-start | bytes 393224 | tf_op jit(solution)/shard_map/ppermute | solution.py:282
  71.5 15.6 %collective-permute-start.10 = (bf16[32,2048]{1,0:T(8,128)(2,1)}, bf16[32,2048]{1,0:T(8,128)(2,1)S(1)}, u32[]{:S(2)}, u32[]{:S(2)}) collective-permute-start(bf16[32,2048]{1,0:T(8,128)(2,1)} %get-tuple-element.33.current_ref), channel_id=1, source_target_pairs={{0,2},{2,4},{4,6},{6,8},{8,10},{10,12},{12,14},{14,16},{16,18},{18... | collective-permute-start | bytes 393224 | tf_op jit(solution)/shard_map/ppermute | solution.py:281
  82.9 10.1 %collective-permute-start.7 = (bf16[8,32,128]{2,1,0:T(8,128)(2,1)S(1)}, bf16[8,32,128]{2,1,0:T(8,128)(2,1)S(1)}, u32[]{:S(2)}, u32[]{:S(2)}) collective-permute-start(bf16[8,32,128]{2,1,0:T(8,128)(2,1)S(1)} %get-tuple-element.30), channel_id=1, source_target_pairs={{0,2},{2,4},{4,6},{6,0},{1,3},{3,5},{5,7},{7,1},{8,10},{10,12},{12... | collective-permute-start | bytes 196616 | tf_op jit(solution)/shard_map/ppermute | solution.py:294
  84.1 9.0 %collective-permute-start.8 = (bf16[8,32,128]{2,1,0:T(8,128)(2,1)S(1)}, bf16[8,32,128]{2,1,0:T(8,128)(2,1)S(1)}, u32[]{:S(2)}, u32[]{:S(2)}) collective-permute-start(bf16[8,32,128]{2,1,0:T(8,128)(2,1)S(1)} %get-tuple-element.31), channel_id=1, source_target_pairs={{0,6},{2,0},{4,2},{6,4},{1,7},{3,1},{5,3},{7,5},{8,14},{10,8},{12,... | collective-permute-start | bytes 196616 | tf_op jit(solution)/shard_map/ppermute | solution.py:294
  86.2 6.8 %collective-permute-start.9 = (bf16[8,32,128]{2,1,0:T(8,128)(2,1)S(1)}, bf16[8,32,128]{2,1,0:T(8,128)(2,1)S(1)}, u32[]{:S(2)}, u32[]{:S(2)}) collective-permute-start(bf16[8,32,128]{2,1,0:T(8,128)(2,1)S(1)} %get-tuple-element.32), channel_id=1, source_target_pairs={{0,4},{2,6},{4,0},{6,2},{1,5},{3,7},{5,1},{7,3},{8,12},{10,14},{12... | collective-permute-start | bytes 196616 | tf_op jit(solution)/shard_map/ppermute | solution.py:294

commit v4 on v3

--- a/solution.py
+++ b/solution.py
@@ -148,10 +148,11 @@
     for c in range(clusters):
         at = width + c * leaf
         total = 0.5 * window[:, at : at + leaf].astype(jnp.float32)
+        copies[2 * c].wait()
+        copies[2 * c + 1].wait()
         for k, (cols, held) in enumerate(((here, a_held), (there, b_held))):
-            copies[2 * c + k].wait()
             for s in range(slots):
-                block = turned.at[c % 2, k * slots + s]
+                block = turned.at[c % 4, k * slots + s]
                 block[...] = held[c, s].T
                 start = pl.multiple_of((cols[s, c] - first) * leaf, leaf)
                 total = total + product(window[:, pl.ds(start, leaf)], block[...], NN)
@@ -170,10 +171,10 @@
             pltpu.VMEM((cols, 3 * width), current.dtype),
             pltpu.VMEM(a.shape, a.dtype),
             pltpu.VMEM(b.shape, b.dtype),
-            pltpu.VMEM((2, 2 * slots, leaf, leaf), a.dtype),
+            pltpu.VMEM((4, 2 * slots, leaf, leaf), a.dtype),
             pltpu.SemaphoreType.DMA((2 * clusters + 1,)),
         ],
-        compiler_params=params(16),
+        compiler_params=params(20),
         cost_estimate=cost(4 * clusters * slots * cols * leaf * leaf, 9_000_000),
         name="near",
     )(first, here, there, before, after, in_hbm(current), in_hbm(a), in_hbm(b))

time: 94.8 us -> 94.2 us (level)
  transfers between devices with their start and end apart: 15 -> 15, of which waited for: 3 -> 3; matrix products, arithmetic and copies ran while one was open for 3% -> 3% of each run, Pallas kernels for 21% -> 20%
where the time goes in v4:
time: 94.2 us; the launch traced here: 93.4 us
  starting transfers between devices  47.6 us (51%)
  Pallas kernels  22.8 us (24%)
  waiting for transfers between devices  19.5 us (21%)
  local copies, waits for them, and re-layouts  1.39 us (1%)
  matrix products  1.32 us (1%)
    all_to_all x2, waiting for transfers between devices, exchanges(): picked = lax.all_to_all(blocks, 'row', 0, 0, tiled=True)  12.3 us
    ppermute x2, starting transfers between devices, exchanges(): after = lax.ppermute(current, ('row', 'col'), down)  11.7 us
    pallas_call x2, Pallas kernels, near_terms(): pl.pallas_call(near_kernel, out_shape=jax.ShapeDtypeStruct((clusters, col...  11.2 us
    all_to_all x1, starting transfers between devices, per_device(): lax.all_to_all(far_src.reshape(row_peers, 1, slot_count), 'row', 0, 0, ti...  11.2 us
    all_to_all x2, starting transfers between devices, exchanges(): picked = lax.all_to_all(blocks, 'row', 0, 0, tiled=True)  10.8 us
    ppermute x6, starting transfers between devices, exchanges(): moved.append(lax.ppermute(part, 'col', ring))  9.49 us
    all_to_all x1, waiting for transfers between devices, per_device(): lax.all_to_all(far_src.reshape(row_peers, 1, slot_count), 'row', 0, 0, ti...  7.17 us
    ppermute x2, starting transfers between devices, exchanges(): before = lax.ppermute(current, ('row', 'col'), up)  3.84 us
  transfers between devices with their start and end apart: 15, of which 3 were waited for; matrix products, arithmetic and copies ran while one was open for 3% of the time, Pallas kernels for 20%

profile of v4, /device:TPU:32, one launch (start us, length us, event | category | flops | bytes accessed | tf_op | source)
XLA Modules:
  0.0 93.4 jit_solution(17227167462154718439)
XLA Ops:
  0.6 0.1 collective-permute-start.6
  0.7 0.5 collective-permute-start
  1.2 1.4 %copy.10 = s32[32,1,2]{2,1,0:T(1,128)} copy(s32[32,1,2]{0,2,1:T(2,128)} %bitcast.27) | data formatting | bytes 512 | tf_op jit(solution)/shard_map/reshape | solution.py:259
  2.6 11.2 %all-to-all-start = ((s32[32,1,2]{2,1,0:T(1,128)}), s32[32,1,2]{2,1,0:T(1,128)S(1)}, u32[]{:S(2)}, u32[]{:S(2)}) async-start(s32[32,1,2]{2,1,0:T(1,128)} %copy.10), calls=%async_computation | async-start | bytes 32768 | tf_op jit(solution)/shard_map/all_to_all | solution.py:259
  13.8 1.3 %convolution_convert_fusion.coeffs_ref = bf16[8,32,128]{2,1,0:T(8,128)(2,1)S(1)} fusion(bf16[8,256,128]{2,1,0:T(8,128)(2,1)} %refs_5_.1, bf16[4,8,8,256]{3,2,1,0:T(8,128)(2,1)} %bitcast.25), kind=kOutput, calls=%fused_computation | convolution fusion | flops 16809984 | bytes 720896 | tf_op jit(solution)/shard_map/sao,aon->asn/dot_general | solution.py:272
  15.1 0.0 copy-start.2
  15.2 7.2 %all-to-all-done.wanted_ref = s32[32,1,2]{2,1,0:T(1,128)S(1)} async-done(((s32[32,1,2]{2,1,0:T(1,128)}), s32[32,1,2]{2,1,0:T(1,128)S(1)}, u32[]{:S(2)}, u32[]{:S(2)}) %all-to-all-start) | async-done | bytes 288 | tf_op jit(solution)/shard_map/all_to_all | solution.py:259
  22.3 1.7 %pick.1 = bf16[64,32,128]{2,1,0:T(8,128)(2,1)} custom-call(s32[32,1,2]{2,1,0:T(1,128)S(1)} %all-to-all-done.wanted_ref, bf16[8,32,128]{2,1,0:T(8,128)(2,1)S(1)} %convolution_convert_fusion.coeffs_ref), custom_call_target="tpu_custom_call" | custom-call | bytes 600000 | tf_op jit(solution)/shard_map/pick/pallas_call | solution.py:83
  24.0 4.9 %all-to-all-start.1 = ((bf16[32,64,128]{2,1,0:T(8,128)(2,1)}), bf16[32,64,128]{2,1,0:T(8,128)(2,1)S(1)}, u32[]{:S(2)}, u32[]{:S(2)}) async-start(bf16[32,64,128]{2,1,0:T(8,128)(2,1)} %bitcast.5), calls=%async_computation.1 | async-start | bytes 1048576 | tf_op jit(solution)/shard_map/all_to_all | solution.py:285
  28.9 7.0 %collective-permute-start.5 = (bf16[32,2048]{1,0:T(8,128)(2,1)}, bf16[32,2048]{1,0:T(8,128)(2,1)S(1)}, u32[]{:S(2)}, u32[]{:S(2)}) collective-permute-start(bf16[32,2048]{1,0:T(8,128)(2,1)} %current_ref), channel_id=1, source_target_pairs={{2,0},{4,2},{6,4},{8,6},{10,8},{12,10},{14,12},{16,14},{18,16},{20... | collective-permute-start | bytes 393224 | tf_op jit(solution)/shard_map/ppermute | solution.py:283
  36.0 1.9 %collective-permute-start.4 = (bf16[32,2048]{1,0:T(8,128)(2,1)}, bf16[32,2048]{1,0:T(8,128)(2,1)S(1)}, u32[]{:S(2)}, u32[]{:S(2)}) collective-permute-start(bf16[32,2048]{1,0:T(8,128)(2,1)} %current_ref), channel_id=1, source_target_pairs={{0,2},{2,4},{4,6},{6,8},{8,10},{10,12},{12,14},{14,16},{16,18},{18... | collective-permute-start | bytes 393224 | tf_op jit(solution)/shard_map/ppermute | solution.py:282
  37.9 3.4 %stage.1.couple_ref = bf16[32,2,128,128]{3,2,1,0:T(8,128)(2,1)S(1)} custom-call(bf16[32,2,128,128]{3,2,1,0:T(8,128)(2,1)} %bitcast.24), custom_call_target="tpu_custom_call" | custom-call | bytes 4194304 | tf_op jit(solution)/shard_map/stage/pallas_call | solution.py:57
  41.3 4.1 %all-to-all-done.1 = bf16[32,64,128]{2,1,0:T(8,128)(2,1)S(1)} async-done(((bf16[32,64,128]{2,1,0:T(8,128)(2,1)}), bf16[32,64,128]{2,1,0:T(8,128)(2,1)S(1)}, u32[]{:S(2)}, u32[]{:S(2)}) %all-to-all-start.1) | async-done | bytes 524320 | tf_op jit(solution)/shard_map/all_to_all | solution.py:285
  45.4 1.3 %couple.2 = (f32[8,32,128]{2,1,0:T(8,128)S(1)}, bf16[8,32,128]{2,1,0:T(8,128)(2,1)S(1)}, bf16[8,32,128]{2,1,0:T(8,128)(2,1)S(1)}, bf16[8,32,128]{2,1,0:T(8,128)(2,1)S(1)}) custom-call(s32[1]{0:T(128)} %bitcast.2.place_ref, s32[2,32]{1,0:T(2,128)S(1)} %bitcast.22, bf16[64,32,128]{2,1,0:T(8,128)(2,1)S(1)} %bitcast.17, ...), custom_call_target="tpu_custom_call" | custom-call | flops 67108864 | bytes 4000000 | tf_op jit(solution)/shard_map/couple/pallas_call | solution.py:114
  46.7 1.6 %collective-permute-start.1 = (bf16[8,32,128]{2,1,0:T(8,128)(2,1)S(1)}, bf16[8,32,128]{2,1,0:T(8,128)(2,1)S(1)}, u32[]{:S(2)}, u32[]{:S(2)}) collective-permute-start(bf16[8,32,128]{2,1,0:T(8,128)(2,1)S(1)} %get-tuple-element.21), channel_id=1, source_target_pairs={{0,2},{2,4},{4,6},{6,0},{1,3},{3,5},{5,7},{7,1},{8,10},{10,12},{12... | collective-permute-start | bytes 196616 | tf_op jit(solution)/shard_map/ppermute | solution.py:295
  48.3 1.7 %collective-permute-start.2 = (bf16[8,32,128]{2,1,0:T(8,128)(2,1)S(1)}, bf16[8,32,128]{2,1,0:T(8,128)(2,1)S(1)}, u32[]{:S(2)}, u32[]{:S(2)}) collective-permute-start(bf16[8,32,128]{2,1,0:T(8,128)(2,1)S(1)} %get-tuple-element.22), channel_id=1, source_target_pairs={{0,6},{2,0},{4,2},{6,4},{1,7},{3,1},{5,3},{7,5},{8,14},{10,8},{12,... | collective-permute-start | bytes 196616 | tf_op jit(solution)/shard_map/ppermute | solution.py:295
  50.0 0.0 collective-permute-done.5.after
  50.0 2.0 %collective-permute-start.3 = (bf16[8,32,128]{2,1,0:T(8,128)(2,1)S(1)}, bf16[8,32,128]{2,1,0:T(8,128)(2,1)S(1)}, u32[]{:S(2)}, u32[]{:S(2)}) collective-permute-start(bf16[8,32,128]{2,1,0:T(8,128)(2,1)S(1)} %get-tuple-element.23), channel_id=1, source_target_pairs={{0,4},{2,6},{4,0},{6,2},{1,5},{3,7},{5,1},{7,3},{8,12},{10,14},{12... | collective-permute-start | bytes 196616 | tf_op jit(solution)/shard_map/ppermute | solution.py:295
  52.0 0.0 copy-start
  52.0 0.0 copy-start.1
  52.0 5.6 %near.2.refs_4_ = f32[8,32,256]{2,1,0:T(8,128)S(1)} custom-call(s32[1]{0:T(128)} %bitcast.8.first_ref, s32[4,8]{1,0:T(4,128)S(1)} %bitcast.20, s32[4,8]{1,0:T(4,128)S(1)} %collective-permute-done.there, bf16[32,2048]{1,0:T(8,128)(2,1)S(1)} %collective-permute-done.4.before, bf16[32,2048]{1,0:T(8,128)(2,1)S(1)} %collective-permute-done.5.after, ...), custom_call_target="tpu_custom_call" | custom-call | flops 268435456 | bytes 9000000 | tf_op jit(solution)/shard_map/near/pallas_call | solution.py:165
  57.7 3.0 %finish_and_pick.1 = (bf16[32,2048]{1,0:T(8,128)(2,1)}, bf16[64,32,128]{2,1,0:T(8,128)(2,1)}) custom-call(s32[32,1,2]{2,1,0:T(1,128)S(1)} %all-to-all-done.wanted_ref, f32[8,32,128]{2,1,0:T(8,128)S(1)} %get-tuple-element.20.own, bf16[8,32,128]{2,1,0:T(8,128)(2,1)S(1)} %collective-permute-done.1.refs_0_, ...), custom_call_target="tpu_custom_call" | custom-call | flops 40000000 | bytes 2500000 | tf_op jit(solution)/shard_map/finish_and_pick/pallas_call | solution.py:228
  60.7 5.9 %all-to-all-start.2 = ((bf16[32,64,128]{2,1,0:T(8,128)(2,1)}), bf16[32,64,128]{2,1,0:T(8,128)(2,1)S(1)}, u32[]{:S(2)}, u32[]{:S(2)}) async-start(bf16[32,64,128]{2,1,0:T(8,128)(2,1)} %bitcast.26), calls=%async_computation.2 | async-start | bytes 1048576 | tf_op jit(solution)/shard_map/all_to_all | solution.py:285
  66.6 4.6 %collective-permute-start.11 = (bf16[32,2048]{1,0:T(8,128)(2,1)}, bf16[32,2048]{1,0:T(8,128)(2,1)S(1)}, u32[]{:S(2)}, u32[]{:S(2)}) collective-permute-start(bf16[32,2048]{1,0:T(8,128)(2,1)} %get-tuple-element.33.current_ref), channel_id=1, source_target_pairs={{2,0},{4,2},{6,4},{8,6},{10,8},{12,10},{14,12},{16,14},{18,16},{20... | collective-permute-start | bytes 393224 | tf_op jit(solution)/shard_map/ppermute | solution.py:283
  71.2 1.9 %collective-permute-start.10 = (bf16[32,2048]{1,0:T(8,128)(2,1)}, bf16[32,2048]{1,0:T(8,128)(2,1)S(1)}, u32[]{:S(2)}, u32[]{:S(2)}) collective-permute-start(bf16[32,2048]{1,0:T(8,128)(2,1)} %get-tuple-element.33.current_ref), channel_id=1, source_target_pairs={{0,2},{2,4},{4,6},{6,8},{8,10},{10,12},{12,14},{14,16},{16,18},{18... | collective-permute-start | bytes 393224 | tf_op jit(solution)/shard_map/ppermute | solution.py:282
  73.1 8.2 %all-to-all-done.2 = bf16[32,64,128]{2,1,0:T(8,128)(2,1)S(1)} async-done(((bf16[32,64,128]{2,1,0:T(8,128)(2,1)}), bf16[32,64,128]{2,1,0:T(8,128)(2,1)S(1)}, u32[]{:S(2)}, u32[]{:S(2)}) %all-to-all-start.2) | async-done | bytes 524320 | tf_op jit(solution)/shard_map/all_to_all | solution.py:285
  81.4 1.3 %couple.3 = (f32[8,32,128]{2,1,0:T(8,128)S(1)}, bf16[8,32,128]{2,1,0:T(8,128)(2,1)S(1)}, bf16[8,32,128]{2,1,0:T(8,128)(2,1)S(1)}, bf16[8,32,128]{2,1,0:T(8,128)(2,1)S(1)}) custom-call(s32[1]{0:T(128)} %bitcast.2.place_ref, s32[2,32]{1,0:T(2,128)S(1)} %bitcast.23, bf16[64,32,128]{2,1,0:T(8,128)(2,1)S(1)} %bitcast.18, ...), custom_call_target="tpu_custom_call" | custom-call | flops 67108864 | bytes 4000000 | tf_op jit(solution)/shard_map/couple/pallas_call | solution.py:114
  82.6 1.1 %collective-permute-start.7 = (bf16[8,32,128]{2,1,0:T(8,128)(2,1)S(1)}, bf16[8,32,128]{2,1,0:T(8,128)(2,1)S(1)}, u32[]{:S(2)}, u32[]{:S(2)}) collective-permute-start(bf16[8,32,128]{2,1,0:T(8,128)(2,1)S(1)} %get-tuple-element.30), channel_id=1, source_target_pairs={{0,2},{2,4},{4,6},{6,0},{1,3},{3,5},{5,7},{7,1},{8,10},{10,12},{12... | collective-permute-start | bytes 196616 | tf_op jit(solution)/shard_map/ppermute | solution.py:295
  83.8 2.2 %collective-permute-start.8 = (bf16[8,32,128]{2,1,0:T(8,128)(2,1)S(1)}, bf16[8,32,128]{2,1,0:T(8,128)(2,1)S(1)}, u32[]{:S(2)}, u32[]{:S(2)}) collective-permute-start(bf16[8,32,128]{2,1,0:T(8,128)(2,1)S(1)} %get-tuple-element.31), channel_id=1, source_target_pairs={{0,6},{2,0},{4,2},{6,4},{1,7},{3,1},{5,3},{7,5},{8,14},{10,8},{12,... | collective-permute-start | bytes 196616 | tf_op jit(solution)/shard_map/ppermute | solution.py:295
  85.9 0.9 collective-permute-start.9
  86.8 5.6 %near.3.refs_4_ = f32[8,32,256]{2,1,0:T(8,128)S(1)} custom-call(s32[1]{0:T(128)} %bitcast.8.first_ref, s32[4,8]{1,0:T(4,128)S(1)} %bitcast.21, s32[4,8]{1,0:T(4,128)S(1)} %collective-permute-done.there, bf16[32,2048]{1,0:T(8,128)(2,1)S(1)} %collective-permute-done.10.before, bf16[32,2048]{1,0:T(8,128)(2,1)S(1)} %collective-permute-done.11.after, ...), custom_call_target="tpu_custom_call" | custom-call | flops 268435456 | bytes 9000000 | tf_op jit(solution)/shard_map/near/pallas_call | solution.py:165
  92.5 0.9 %finish.1 = bf16[32,2048]{1,0:T(8,128)(2,1)} custom-call(f32[8,32,128]{2,1,0:T(8,128)S(1)} %get-tuple-element.29.own, bf16[8,32,128]{2,1,0:T(8,128)(2,1)S(1)} %collective-permute-done.7.refs_0_, bf16[8,32,128]{2,1,0:T(8,128)(2,1)S(1)} %collective-permute-done.8.refs_1_, bf16[8,32,128]{2,1,0:T(8,128)(2,1)S(1)} %collective-permute-done.9.refs_2_, ...), custom_call_target="tpu_custom_call" | custom-call | flops 20000000 | bytes 1500000 | tf_op jit(solution)/shard_map/finish/pallas_call | solution.py:213
  (16 shorter events, 0.0 us)
Async XLA Ops:
  0.6 44.8 %copy-start.3 = (s32[1,1,32,2]{2,3,1,0:T(2,128)S(1)}, s32[1,1,32,2]{2,3,1,0:T(2,128)}, u32[]{:S(2)}) copy-start(s32[1,1,32,2]{2,3,1,0:T(2,128)} %param.12) | copy-start | bytes 772
  0.6 51.3 %collective-permute-start.6 = (bf16[8,4,256,256]{3,2,1,0:T(8,128)(2,1)}, bf16[8,4,256,256]{3,2,1,0:T(8,128)(2,1)}, u32[]{:S(2)}, u32[]{:S(2)}) collective-permute-start(bf16[8,4,256,256]{3,2,1,0:T(8,128)(2,1)} %a_ref.3), channel_id=1, source_target_pairs={{0,1},{1,0},{2,3},{3,2},{4,5},{5,4},{6,7},{7,6},{8,9},{9,8},{10,11... | collective-permute-start | bytes 12582920 | tf_op jit(solution)/shard_map/ppermute | solution.py:276
  0.7 14.4 %collective-permute-start = (s32[4,8]{1,0:T(4,128)}, s32[4,8]{1,0:T(4,128)S(1)}, u32[]{:S(2)}, u32[]{:S(2)}) collective-permute-start(s32[4,8]{1,0:T(4,128)} %bitcast.19), channel_id=1, source_target_pairs={{0,1},{1,0},{2,3},{3,2},{4,5},{5,4},{6,7},{7,6},{8,9},{9,8},{10,11... | collective-permute-start | bytes 392 | tf_op jit(solution)/shard_map/ppermute | solution.py:264
  2.6 19.7 %all-to-all-start = ((s32[32,1,2]{2,1,0:T(1,128)}), s32[32,1,2]{2,1,0:T(1,128)S(1)}, u32[]{:S(2)}, u32[]{:S(2)}) async-start(s32[32,1,2]{2,1,0:T(1,128)} %copy.10), calls=%async_computation | async-start | bytes 32768 | tf_op jit(solution)/shard_map/all_to_all | solution.py:259
  15.1 36.8 %copy-start.2 = (s32[8,4]{0,1:T(4,128)S(1)}, s32[8,4]{0,1:T(4,128)}, u32[]{:S(2)}) copy-start(s32[8,4]{0,1:T(4,128)} %param.10) | copy-start | bytes 388
  24.0 21.4 %all-to-all-start.1 = ((bf16[32,64,128]{2,1,0:T(8,128)(2,1)}), bf16[32,64,128]{2,1,0:T(8,128)(2,1)S(1)}, u32[]{:S(2)}, u32[]{:S(2)}) async-start(bf16[32,64,128]{2,1,0:T(8,128)(2,1)} %bitcast.5), calls=%async_computation.1 | async-start | bytes 1048576 | tf_op jit(solution)/shard_map/all_to_all | solution.py:285
  28.9 21.1 %collective-permute-start.5 = (bf16[32,2048]{1,0:T(8,128)(2,1)}, bf16[32,2048]{1,0:T(8,128)(2,1)S(1)}, u32[]{:S(2)}, u32[]{:S(2)}) collective-permute-start(bf16[32,2048]{1,0:T(8,128)(2,1)} %current_ref), channel_id=1, source_target_pairs={{2,0},{4,2},{6,4},{8,6},{10,8},{12,10},{14,12},{16,14},{18,16},{20... | collective-permute-start | bytes 393224 | tf_op jit(solution)/shard_map/ppermute | solution.py:283
  36.0 16.0 %collective-permute-start.4 = (bf16[32,2048]{1,0:T(8,128)(2,1)}, bf16[32,2048]{1,0:T(8,128)(2,1)S(1)}, u32[]{:S(2)}, u32[]{:S(2)}) collective-permute-start(bf16[32,2048]{1,0:T(8,128)(2,1)} %current_ref), channel_id=1, source_target_pairs={{0,2},{2,4},{4,6},{6,8},{8,10},{10,12},{12,14},{14,16},{16,18},{18... | collective-permute-start | bytes 393224 | tf_op jit(solution)/shard_map/ppermute | solution.py:282
  46.7 11.0 %collective-permute-start.1 = (bf16[8,32,128]{2,1,0:T(8,128)(2,1)S(1)}, bf16[8,32,128]{2,1,0:T(8,128)(2,1)S(1)}, u32[]{:S(2)}, u32[]{:S(2)}) collective-permute-start(bf16[8,32,128]{2,1,0:T(8,128)(2,1)S(1)} %get-tuple-element.21), channel_id=1, source_target_pairs={{0,2},{2,4},{4,6},{6,0},{1,3},{3,5},{5,7},{7,1},{8,10},{10,12},{12... | collective-permute-start | bytes 196616 | tf_op jit(solution)/shard_map/ppermute | solution.py:295
  48.3 9.3 %collective-permute-start.2 = (bf16[8,32,128]{2,1,0:T(8,128)(2,1)S(1)}, bf16[8,32,128]{2,1,0:T(8,128)(2,1)S(1)}, u32[]{:S(2)}, u32[]{:S(2)}) collective-permute-start(bf16[8,32,128]{2,1,0:T(8,128)(2,1)S(1)} %get-tuple-element.22), channel_id=1, source_target_pairs={{0,6},{2,0},{4,2},{6,4},{1,7},{3,1},{5,3},{7,5},{8,14},{10,8},{12,... | collective-permute-start | bytes 196616 | tf_op jit(solution)/shard_map/ppermute | solution.py:295
  50.0 7.7 %collective-permute-start.3 = (bf16[8,32,128]{2,1,0:T(8,128)(2,1)S(1)}, bf16[8,32,128]{2,1,0:T(8,128)(2,1)S(1)}, u32[]{:S(2)}, u32[]{:S(2)}) collective-permute-start(bf16[8,32,128]{2,1,0:T(8,128)(2,1)S(1)} %get-tuple-element.23), channel_id=1, source_target_pairs={{0,4},{2,6},{4,0},{6,2},{1,5},{3,7},{5,1},{7,3},{8,12},{10,14},{12... | collective-permute-start | bytes 196616 | tf_op jit(solution)/shard_map/ppermute | solution.py:295
  52.0 5.7 %copy-start = (bf16[8,256,128]{2,1,0:T(8,128)(2,1)S(1)}, bf16[8,256,128]{2,1,0:T(8,128)(2,1)}, u32[]{:S(2)}) copy-start(bf16[8,256,128]{2,1,0:T(8,128)(2,1)} %refs_5_.1) | copy-start | bytes 1572868
  52.0 5.7 %copy-start.1 = (bf16[8,256,128]{2,1,0:T(8,128)(2,1)S(1)}, bf16[8,256,128]{2,1,0:T(8,128)(2,1)}, u32[]{:S(2)}) copy-start(bf16[8,256,128]{2,1,0:T(8,128)(2,1)} %refs_3_.3) | copy-start | bytes 1572868
  60.7 20.7 %all-to-all-start.2 = ((bf16[32,64,128]{2,1,0:T(8,128)(2,1)}), bf16[32,64,128]{2,1,0:T(8,128)(2,1)S(1)}, u32[]{:S(2)}, u32[]{:S(2)}) async-start(bf16[32,64,128]{2,1,0:T(8,128)(2,1)} %bitcast.26), calls=%async_computation.2 | async-start | bytes 1048576 | tf_op jit(solution)/shard_map/all_to_all | solution.py:285
  66.6 20.2 %collective-permute-start.11 = (bf16[32,2048]{1,0:T(8,128)(2,1)}, bf16[32,2048]{1,0:T(8,128)(2,1)S(1)}, u32[]{:S(2)}, u32[]{:S(2)}) collective-permute-start(bf16[32,2048]{1,0:T(8,128)(2,1)} %get-tuple-element.33.current_ref), channel_id=1, source_target_pairs={{2,0},{4,2},{6,4},{8,6},{10,8},{12,10},{14,12},{16,14},{18,16},{20... | collective-permute-start | bytes 393224 | tf_op jit(solution)/shard_map/ppermute | solution.py:283
  71.2 15.6 %collective-permute-start.10 = (bf16[32,2048]{1,0:T(8,128)(2,1)}, bf16[32,2048]{1,0:T(8,128)(2,1)S(1)}, u32[]{:S(2)}, u32[]{:S(2)}) collective-permute-start(bf16[32,2048]{1,0:T(8,128)(2,1)} %get-tuple-element.33.current_ref), channel_id=1, source_target_pairs={{0,2},{2,4},{4,6},{6,8},{8,10},{10,12},{12,14},{14,16},{16,18},{18... | collective-permute-start | bytes 393224 | tf_op jit(solution)/shard_map/ppermute | solution.py:282
  82.6 9.8 %collective-permute-start.7 = (bf16[8,32,128]{2,1,0:T(8,128)(2,1)S(1)}, bf16[8,32,128]{2,1,0:T(8,128)(2,1)S(1)}, u32[]{:S(2)}, u32[]{:S(2)}) collective-permute-start(bf16[8,32,128]{2,1,0:T(8,128)(2,1)S(1)} %get-tuple-element.30), channel_id=1, source_target_pairs={{0,2},{2,4},{4,6},{6,0},{1,3},{3,5},{5,7},{7,1},{8,10},{10,12},{12... | collective-permute-start | bytes 196616 | tf_op jit(solution)/shard_map/ppermute | solution.py:295
  83.8 8.7 %collective-permute-start.8 = (bf16[8,32,128]{2,1,0:T(8,128)(2,1)S(1)}, bf16[8,32,128]{2,1,0:T(8,128)(2,1)S(1)}, u32[]{:S(2)}, u32[]{:S(2)}) collective-permute-start(bf16[8,32,128]{2,1,0:T(8,128)(2,1)S(1)} %get-tuple-element.31), channel_id=1, source_target_pairs={{0,6},{2,0},{4,2},{6,4},{1,7},{3,1},{5,3},{7,5},{8,14},{10,8},{12,... | collective-permute-start | bytes 196616 | tf_op jit(solution)/shard_map/ppermute | solution.py:295
  85.9 6.5 %collective-permute-start.9 = (bf16[8,32,128]{2,1,0:T(8,128)(2,1)S(1)}, bf16[8,32,128]{2,1,0:T(8,128)(2,1)S(1)}, u32[]{:S(2)}, u32[]{:S(2)}) collective-permute-start(bf16[8,32,128]{2,1,0:T(8,128)(2,1)S(1)} %get-tuple-element.32), channel_id=1, source_target_pairs={{0,4},{2,6},{4,0},{6,2},{1,5},{3,7},{5,1},{7,3},{8,12},{10,14},{12... | collective-permute-start | bytes 196616 | tf_op jit(solution)/shard_map/ppermute | solution.py:295
